TPU v7x, 32 devices: a whole 2x2x4 slice. The times are simulated.
32 devices in a mesh: blk: 4 (over y, core), dp: 8 (over z, x).
Axes of the slice: x: 2, y: 2, z: 4, core: 2. Of those that a mesh axis runs over, the one named last changes fastest.
Arguments:
- tokens: bfloat16 [8, 1024, 384], P('dp', 'blk'), may hold values from -6 to 6
- lengths: int32 [8], P('dp'), may hold values from 512 to 1024, as said below
- query_weight: bfloat16 [384, 384], replicated, may hold values from -0.3125 to 0.3125
- query_bias: bfloat16 [384], replicated, may hold values from -1.5 to 1.5
- key_weight: bfloat16 [384, 384], replicated, may hold values from -0.3125 to 0.3125
- key_bias: bfloat16 [384], replicated, may hold values from -1.5 to 1.5
- value_weight: bfloat16 [384, 384], replicated, may hold values from -0.3125 to 0.3125
- value_bias: bfloat16 [384], replicated, may hold values from -1.5 to 1.5
- output_weight: bfloat16 [384, 384], replicated, may hold values from -2.5 to 2.5
- output_bias: bfloat16 [384], replicated, may hold values from -1.5 to 1.5
- first_gain: bfloat16 [384], replicated, may hold values from 0.5 to 1.5
- first_bias: bfloat16 [384], replicated, may hold values from -1.5 to 1.5
- inner_weight: bfloat16 [384, 1536], replicated, may hold values from -0.3125 to 0.3125
- inner_bias: bfloat16 [1536], replicated, may hold values from -1.5 to 1.5
- outer_weight: bfloat16 [1536, 384], replicated, may hold values from -0.15625 to 0.15625
- outer_bias: bfloat16 [384], replicated, may hold values from -1.5 to 1.5
- second_gain: bfloat16 [384], replicated, may hold values from 0.5 to 1.5
- second_bias: bfloat16 [384], replicated, may hold values from -1.5 to 1.5
- relative_table: bfloat16 [512, 384], replicated, may hold values from -6 to 6
- cotangent: bfloat16 [8, 1024, 384], P('dp', 'blk'), may hold values from -18 to 18
Outputs:
- layer_out: float32 [8, 1024, 384], P('dp', 'blk')
- grad_tokens: float32 [8, 1024, 384], P('dp', 'blk')
- grad_query_weight: float32 [384, 384], replicated
- grad_query_bias: float32 [384], replicated
- grad_key_weight: float32 [384, 384], replicated
- grad_key_bias: float32 [384], replicated
- grad_value_weight: float32 [384, 384], replicated
- grad_value_bias: float32 [384], replicated
- grad_output_weight: float32 [384, 384], replicated
- grad_output_bias: float32 [384], replicated
- grad_first_gain: float32 [384], replicated
- grad_first_bias: float32 [384], replicated
- grad_inner_weight: float32 [384, 1536], replicated
- grad_inner_bias: float32 [1536], replicated
- grad_outer_weight: float32 [1536, 384], replicated
- grad_outer_bias: float32 [384], replicated
- grad_second_gain: float32 [384], replicated
- grad_second_bias: float32 [384], replicated
- grad_relative_table: float32 [512, 384], replicated
Inputs may be any that keep to these rules, and one draw needn't show every extreme that they name: `lengths`: one sequence uses all 1024 positions and one uses 1024 // 2.
All inputs are finite; a program needn't handle non-finite values.
Results may differ from a plain program's by a relative error of at most 0.04.
Values may be sent and summed in bfloat16 or wider, within the bound.
No kernel may reach another device: no remote copies, remote signals or barrier semaphores. Data moves between devices by JAX's collectives and lax.ppermute only.
A program may use at most 320 MiB of HBM per device.

v0:
```python
from functools import partial
import math

import jax
import jax.numpy as jnp
from jax import lax
from jax.sharding import PartitionSpec as P

HEADS = 6


def layer_norm(values, gain_vec, bias_vec):
    center = values - jnp.mean(values, axis=-1, keepdims=True)
    spread = jnp.mean(center * center, axis=-1, keepdims=True)
    return center * lax.rsqrt(spread + 1e-07) * gain_vec + bias_vec


def skewed(source_table, row_count, col_count):
    table_width = row_count + col_count - 1
    leading = source_table.shape[:-2]
    padded = jnp.pad(source_table, [(0, 0)] * (source_table.ndim - 1) + [(0, 1)])
    flattened = padded.reshape(leading + (row_count * (table_width + 1),))
    flattened = flattened[..., row_count - 1 : row_count - 1 + row_count * table_width]
    return flattened.reshape(leading + (row_count, table_width))[..., :col_count]


def band_terms(query_table, key_table, band_shift):
    row_count = query_table.shape[2]
    col_count = key_table.shape[2]
    last_index = query_table.shape[3] - 1
    steps_along = jnp.arange(row_count + col_count - 1, dtype=jnp.int32)
    query_index = jnp.clip(band_shift + (row_count - 1) - steps_along, 0, last_index)
    to_position = skewed(jnp.take(query_table, query_index, axis=3), row_count, col_count)
    key_index = jnp.clip(band_shift - (col_count - 1) + steps_along, 0, last_index)
    from_position = skewed(jnp.take(key_table, key_index, axis=3), col_count, row_count)
    return to_position + jnp.swapaxes(from_position, 2, 3)


def split_einsum(formula, wide_values, narrow_values):
    upper_part = wide_values.astype(jnp.bfloat16)
    lower_part = (wide_values - upper_part.astype(jnp.float32)).astype(jnp.bfloat16)
    return jnp.einsum(
        formula, upper_part, narrow_values, preferred_element_type=jnp.float32
    ) + jnp.einsum(formula, lower_part, narrow_values, preferred_element_type=jnp.float32)


def project(values, weight, bias_vec):
    return jnp.dot(values, weight, preferred_element_type=jnp.float32) + bias_vec.astype(
        jnp.float32
    )


def weight_grad(left_rows, right_rows):
    return jnp.einsum("sbi,sbo->io", left_rows, right_rows, preferred_element_type=jnp.float32)


def bias_grad(grad_rows):
    return jnp.sum(grad_rows.astype(jnp.float32), axis=(0, 1))


def back_through(grad_rows, weight):
    return jnp.einsum("sbo,io->sbi", grad_rows, weight, preferred_element_type=jnp.float32)


def on_device(
    tokens,
    lengths,
    query_weight,
    query_bias,
    key_weight,
    key_bias,
    value_weight,
    value_bias,
    output_weight,
    output_bias,
    first_gain,
    first_bias,
    inner_weight,
    inner_bias,
    outer_weight,
    outer_bias,
    second_gain,
    second_bias,
    relative_table,
    cotangent,
):
    seq_count, row_count, model_width = tokens.shape
    head_dim = model_width // HEADS
    rel_count = relative_table.shape[0]
    span_half = rel_count // 2
    score_scale = 1.0 / math.sqrt(3.0 * head_dim)
    block_count = lax.axis_size("blk")
    block_index = lax.axis_index("blk")
    first_row = block_index * row_count
    query_rows = project(tokens, query_weight, query_bias).astype(jnp.bfloat16)
    key_rows = project(tokens, key_weight, key_bias).astype(jnp.bfloat16)
    value_rows = project(tokens, value_weight, value_bias).astype(jnp.bfloat16)
    rel_keys = (
        project(relative_table, key_weight, key_bias)
        .astype(jnp.bfloat16)
        .reshape(rel_count, HEADS, head_dim)
    )
    rel_queries = (
        project(relative_table, query_weight, query_bias)
        .astype(jnp.bfloat16)
        .reshape(rel_count, HEADS, head_dim)
    )
    query_heads = query_rows.reshape(seq_count, row_count, HEADS, head_dim)
    query_table = jnp.einsum(
        "sihd,rhd->shir", query_heads, rel_keys, preferred_element_type=jnp.float32
    )

    def block_scores(key_block, offset, with_pull):
        block_len = key_block.shape[1]
        key_heads = key_block.reshape(seq_count, block_len, HEADS, head_dim)
        content = jnp.einsum(
            "sihd,sjhd->shij", query_heads, key_heads, preferred_element_type=jnp.float32
        )
        key_table = jnp.einsum(
            "sjhd,rhd->shjr", key_heads, rel_queries, preferred_element_type=jnp.float32
        )
        band_shift = first_row - offset + span_half
        if with_pull:
            band_part, band_pull = jax.vjp(
                lambda left_table, right_table: band_terms(left_table, right_table, band_shift),
                query_table,
                key_table,
            )
        else:
            band_part = band_terms(query_table, key_table, band_shift)
            band_pull = None
        key_mask = (offset + jnp.arange(block_len, dtype=jnp.int32))[None, :] < lengths[:, None]
        key_mask = key_mask[:, None, None, :]
        scores = jnp.where(key_mask, (content + band_part) * score_scale, -1e30)
        return (scores, key_mask, key_heads, band_pull)

    block_ids = jnp.arange(block_count, dtype=jnp.int32)
    running_max = jnp.full((seq_count, HEADS, row_count), -1e30, jnp.float32)
    scores, key_mask, key_heads, unused_pull = block_scores(
        lax.all_gather(key_rows, "blk", axis=1, tiled=True), jnp.int32(0), False
    )
    next_max = jnp.maximum(running_max, jnp.max(scores, axis=-1))
    weights_now = jnp.where(key_mask, jnp.exp(scores - next_max[..., None]), 0.0)
    denominator = jnp.sum(weights_now, axis=-1)
    running_max, denominator = (next_max, denominator)
    log_total = running_max + jnp.log(denominator)
    scores, key_mask, key_heads, unused_pull = block_scores(
        lax.all_gather(key_rows, "blk", axis=1, tiled=True), jnp.int32(0), False
    )
    value_heads = lax.all_gather(value_rows, "blk", axis=1, tiled=True).reshape(key_heads.shape)
    chances = jnp.where(key_mask, jnp.exp(scores - log_total[..., None]), 0.0)
    weighted = jnp.einsum(
        "shij,sjhd->shid",
        chances.astype(jnp.bfloat16),
        value_heads,
        preferred_element_type=jnp.float32,
    )
    mixture = jnp.transpose(weighted, (0, 2, 1, 3)).reshape(seq_count, row_count, model_width)
    mixture_low = mixture.astype(jnp.bfloat16)
    branch_out = project(mixture_low, output_weight, output_bias)
    first_sum = tokens.astype(jnp.float32) + branch_out
    normed_f, first_pull = jax.vjp(
        layer_norm, first_sum, first_gain.astype(jnp.float32), first_bias.astype(jnp.float32)
    )
    normed = normed_f.astype(jnp.bfloat16)
    inner_pre = project(normed, inner_weight, inner_bias)
    active_f, gelu_pull = jax.vjp(partial(jax.nn.gelu, approximate=False), inner_pre)
    active = active_f.astype(jnp.bfloat16)
    outer_out = project(active, outer_weight, outer_bias)
    second_sum = normed.astype(jnp.float32) + outer_out
    result_f, second_pull = jax.vjp(
        layer_norm, second_sum, second_gain.astype(jnp.float32), second_bias.astype(jnp.float32)
    )
    grad_second, g_second_gain, g_second_bias = second_pull(cotangent.astype(jnp.float32))
    grad_outer = grad_second.astype(jnp.bfloat16)
    g_outer_weight = weight_grad(active, grad_outer)
    g_outer_bias = bias_grad(grad_outer)
    grad_inner = gelu_pull(back_through(grad_outer, outer_weight))[0].astype(jnp.bfloat16)
    g_inner_weight = weight_grad(normed, grad_inner)
    g_inner_bias = bias_grad(grad_inner)
    grad_normed = (back_through(grad_inner, inner_weight) + grad_second).astype(jnp.bfloat16)
    grad_first, g_first_gain, g_first_bias = first_pull(grad_normed.astype(jnp.float32))
    grad_branch = grad_first.astype(jnp.bfloat16)
    g_output_weight = weight_grad(mixture_low, grad_branch)
    g_output_bias = bias_grad(grad_branch)
    grad_mixture = back_through(grad_branch, output_weight).astype(jnp.bfloat16)
    grad_heads = grad_mixture.reshape(seq_count, row_count, HEADS, head_dim)
    row_delta = jnp.transpose(
        jnp.sum(grad_heads.astype(jnp.float32) * mixture.reshape(grad_heads.shape), axis=-1),
        (0, 2, 1),
    )
    key_all, value_all = (
        lax.all_gather(key_rows, "blk", axis=1, tiled=True),
        lax.all_gather(value_rows, "blk", axis=1, tiled=True),
    )

    def back_step(running, block_id):
        grad_query, grad_table, grad_rel_query = running
        offset = block_id * row_count
        key_block = lax.dynamic_slice_in_dim(key_all, offset, row_count, 1)
        value_block = lax.dynamic_slice_in_dim(value_all, offset, row_count, 1)
        scores, key_mask, key_heads, band_pull = block_scores(key_block, offset, True)
        value_heads = value_block.reshape(key_heads.shape)
        chances = jnp.where(key_mask, jnp.exp(scores - log_total[..., None]), 0.0)
        grad_chances = jnp.einsum(
            "sihd,sjhd->shij", grad_heads, value_heads, preferred_element_type=jnp.float32
        )
        grad_scores = (chances * (grad_chances - row_delta[..., None])).astype(jnp.bfloat16)
        grad_values = jnp.einsum(
            "shij,sihd->sjhd",
            chances.astype(jnp.bfloat16),
            grad_heads,
            preferred_element_type=jnp.float32,
        )
        grad_query = grad_query + score_scale * jnp.einsum(
            "shij,sjhd->sihd", grad_scores, key_heads, preferred_element_type=jnp.float32
        )
        grad_keys = score_scale * jnp.einsum(
            "shij,sihd->sjhd", grad_scores, query_heads, preferred_element_type=jnp.float32
        )
        grad_qtab, grad_ktab = band_pull(grad_scores.astype(jnp.float32) * score_scale)
        grad_keys = grad_keys + split_einsum("shjr,rhd->sjhd", grad_ktab, rel_queries)
        grad_rel_query = grad_rel_query + split_einsum("shjr,sjhd->rhd", grad_ktab, key_heads)
        new_state = (grad_query, grad_table + grad_qtab, grad_rel_query)
        return (
            new_state,
            (
                grad_keys.reshape(seq_count, row_count, model_width),
                grad_values.reshape(seq_count, row_count, model_width),
            ),
        )

    back_start = (
        jnp.zeros((seq_count, row_count, HEADS, head_dim), jnp.float32),
        jnp.zeros((seq_count, HEADS, row_count, rel_count), jnp.float32),
        jnp.zeros((rel_count, HEADS, head_dim), jnp.float32),
    )
    back_state, block_grads = lax.scan(back_step, back_start, block_ids)
    key_parts, value_parts = block_grads
    key_home, value_home = (
        lax.psum_scatter(
            key_parts.astype(jnp.bfloat16), "blk", scatter_dimension=0, tiled=True
        ).astype(jnp.float32),
        lax.psum_scatter(
            value_parts.astype(jnp.bfloat16), "blk", scatter_dimension=0, tiled=True
        ).astype(jnp.float32),
    )
    key_home_rows = key_home[0]
    value_home_rows = value_home[0]
    grad_query, grad_table, grad_rel_query = back_state
    grad_key_rows = key_home_rows.astype(jnp.bfloat16)
    grad_value_rows = value_home_rows.astype(jnp.bfloat16)
    grad_query = grad_query + split_einsum("shir,rhd->sihd", grad_table, rel_keys)
    grad_rel_key = split_einsum("shir,sihd->rhd", grad_table, query_heads)
    grad_query_rows = grad_query.reshape(seq_count, row_count, model_width).astype(jnp.bfloat16)
    rel_key_flat = grad_rel_key.reshape(rel_count, model_width)
    rel_query_flat = grad_rel_query.reshape(rel_count, model_width)
    g_query_weight = weight_grad(tokens, grad_query_rows) + split_einsum(
        "ro,ri->io", rel_query_flat, relative_table
    )
    g_query_bias = bias_grad(grad_query_rows) + jnp.sum(rel_query_flat, axis=0)
    g_key_weight = weight_grad(tokens, grad_key_rows) + split_einsum(
        "ro,ri->io", rel_key_flat, relative_table
    )
    g_key_bias = bias_grad(grad_key_rows) + jnp.sum(rel_key_flat, axis=0)
    g_value_weight = weight_grad(tokens, grad_value_rows)
    g_value_bias = bias_grad(grad_value_rows)
    g_relative = split_einsum("ro,io->ri", rel_query_flat, query_weight) + split_einsum(
        "ro,io->ri", rel_key_flat, key_weight
    )
    grad_tokens = (
        back_through(grad_query_rows, query_weight)
        + back_through(grad_key_rows, key_weight)
        + back_through(grad_value_rows, value_weight)
        + grad_first
    )
    (
        g_query_weight,
        g_query_bias,
        g_key_weight,
        g_key_bias,
        g_value_weight,
        g_value_bias,
        g_output_weight,
        g_output_bias,
        g_first_gain,
        g_first_bias,
        g_inner_weight,
        g_inner_bias,
        g_outer_weight,
        g_outer_bias,
        g_second_gain,
        g_second_bias,
        g_relative,
    ) = lax.psum(
        (
            g_query_weight,
            g_query_bias,
            g_key_weight,
            g_key_bias,
            g_value_weight,
            g_value_bias,
            g_output_weight,
            g_output_bias,
            g_first_gain,
            g_first_bias,
            g_inner_weight,
            g_inner_bias,
            g_outer_weight,
            g_outer_bias,
            g_second_gain,
            g_second_bias,
            g_relative,
        ),
        ("blk", "dp"),
    )
    return (
        result_f,
        grad_tokens,
        g_query_weight,
        g_query_bias,
        g_key_weight,
        g_key_bias,
        g_value_weight,
        g_value_bias,
        g_output_weight,
        g_output_bias,
        g_first_gain,
        g_first_bias,
        g_inner_weight,
        g_inner_bias,
        g_outer_weight,
        g_outer_bias,
        g_second_gain,
        g_second_bias,
        g_relative,
    )


def solution(mesh):
    in_specs = (
        P("dp", "blk", None),
        P("dp"),
        P(),
        P(),
        P(),
        P(),
        P(),
        P(),
        P(),
        P(),
        P(),
        P(),
        P(),
        P(),
        P(),
        P(),
        P(),
        P(),
        P(),
        P("dp", "blk", None),
    )
    out_specs = (
        P("dp", "blk", None),
        P("dp", "blk", None),
        P(),
        P(),
        P(),
        P(),
        P(),
        P(),
        P(),
        P(),
        P(),
        P(),
        P(),
        P(),
        P(),
        P(),
        P(),
        P(),
        P(),
    )
    return jax.shard_map(
        on_device, mesh=mesh, in_specs=in_specs, out_specs=out_specs, check_vma=False
    )
```

profile of v0, /device:TPU:9, one launch (start us, length us, event | category | flops | bytes accessed | tf_op | source)
XLA Modules:
  0.0 3079.7 jit_solution(16359634714843966742)
XLA Ops:
  196.5 60.8 %reshape.862 = f32[1,6,1310720]{2,0,1:T(1,128)} reshape(f32[1,6,1024,1280]{3,2,0,1:T(8,128)} %pad.75.clone) | data formatting | bytes 62914560 | tf_op jit(solution)/shard_map/reshape | solution.py:22
  257.3 344.2 %slice_reduce_fusion.2 = f32[6,1309696]{1,0:T(8,128)} fusion(f32[1,6,1310720]{2,0,1:T(1,128)} %reshape.862), kind=kLoop, calls=%fused_computation.65 | loop fusion | bytes 62865408 | tf_op jit(solution)/shard_map/slice | solution.py:23
  601.5 597.2 %while.25 = (u32[]{:T(128)}, f32[1,6,1309696]{2,1,0:T(8,128)}, f32[7858176]{0:T(1024)}, u32[]{}, f32[]{:T(128)}, /*index=5*/u32[]{}, u32[]{}, u32[]{}) while((u32[]{:T(128)}, f32[1,6,1309696]{2,1,0:T(8,128)}, f32[7858176]{0:T(1024)}, u32[]{}, f32[]{:T(128)}, /*index=5*/u32[]{}, u32[]{}, u32[]{}) %tuple.106), condition=%wide.cond, body=%wide.body.sunk | while | flops 9 | bytes 20955336
  602.2 54.1 %dynamic-slice_reduce_fusion.2 = f32[1309696]{0:T(1024)} fusion(f32[]{:T(128)} %broadcast.449, f32[1,6,1309696]{2,1,0:T(8,128)} %get-tuple-element.749, u32[]{:T(128)S(6)} %multiply.58, u32[]{:T(128)S(6)} %multiply.59), kind=kLoop, calls=%fused_computation.219.clone.1 | loop fusion | bytes 10477580
  701.6 54.1 %dynamic-slice_reduce_fusion.2 = f32[1309696]{0:T(1024)} fusion(f32[]{:T(128)} %broadcast.449, f32[1,6,1309696]{2,1,0:T(8,128)} %get-tuple-element.749, u32[]{:T(128)S(6)} %multiply.58, u32[]{:T(128)S(6)} %multiply.59), kind=kLoop, calls=%fused_computation.219.clone.1 | loop fusion | bytes 10477580
  801.1 54.1 %dynamic-slice_reduce_fusion.2 = f32[1309696]{0:T(1024)} fusion(f32[]{:T(128)} %broadcast.449, f32[1,6,1309696]{2,1,0:T(8,128)} %get-tuple-element.749, u32[]{:T(128)S(6)} %multiply.58, u32[]{:T(128)S(6)} %multiply.59), kind=kLoop, calls=%fused_computation.219.clone.1 | loop fusion | bytes 10477580
  900.5 54.1 %dynamic-slice_reduce_fusion.2 = f32[1309696]{0:T(1024)} fusion(f32[]{:T(128)} %broadcast.449, f32[1,6,1309696]{2,1,0:T(8,128)} %get-tuple-element.749, u32[]{:T(128)S(6)} %multiply.58, u32[]{:T(128)S(6)} %multiply.59), kind=kLoop, calls=%fused_computation.219.clone.1 | loop fusion | bytes 10477580
  954.7 44.9 %dynamic-update-slice.2 = f32[7858176]{0:T(1024)} dynamic-update-slice(f32[7858176]{0:T(1024)} %get-tuple-element.742, f32[1309696]{0:T(1024)} %dynamic-slice_reduce_fusion.2, u32[]{:T(128)S(6)} %add.807) | dynamic-update-slice | bytes 10477572
  1000.1 54.1 %dynamic-slice_reduce_fusion.2 = f32[1309696]{0:T(1024)} fusion(f32[]{:T(128)} %broadcast.449, f32[1,6,1309696]{2,1,0:T(8,128)} %get-tuple-element.749, u32[]{:T(128)S(6)} %multiply.58, u32[]{:T(128)S(6)} %multiply.59), kind=kLoop, calls=%fused_computation.219.clone.1 | loop fusion | bytes 10477580
  1054.2 44.9 %dynamic-update-slice.2 = f32[7858176]{0:T(1024)} dynamic-update-slice(f32[7858176]{0:T(1024)} %get-tuple-element.742, f32[1309696]{0:T(1024)} %dynamic-slice_reduce_fusion.2, u32[]{:T(128)S(6)} %add.807) | dynamic-update-slice | bytes 10477572
  1099.7 54.1 %dynamic-slice_reduce_fusion.2 = f32[1309696]{0:T(1024)} fusion(f32[]{:T(128)} %broadcast.449, f32[1,6,1309696]{2,1,0:T(8,128)} %get-tuple-element.749, u32[]{:T(128)S(6)} %multiply.58, u32[]{:T(128)S(6)} %multiply.59), kind=kLoop, calls=%fused_computation.219.clone.1 | loop fusion | bytes 10477580
  1153.8 44.9 %dynamic-update-slice.2 = f32[7858176]{0:T(1024)} dynamic-update-slice(f32[7858176]{0:T(1024)} %get-tuple-element.742, f32[1309696]{0:T(1024)} %dynamic-slice_reduce_fusion.2, u32[]{:T(128)S(6)} %add.807) | dynamic-update-slice | bytes 10477572
  1198.7 61.2 %reshape.993 = f32[6,1,1024,1279]{3,2,1,0:T(8,128)} reshape(f32[7858176]{0:T(1024)} %get-tuple-element.501) | data formatting | bytes 62865408
  1329.6 87.7 %slice_reduce_fusion.3 = f32[6,327424]{1,0:T(8,128)} fusion(f32[1,6,327680]{2,0,1:T(1,128)} %reshape.859), kind=kLoop, calls=%fused_computation.67 | loop fusion | bytes 15716352 | tf_op jit(solution)/shard_map/slice | solution.py:23
  1467.2 1357.7 %while.24 = (s32[]{:T(128)}, f32[1,256,6,64]{1,3,2,0:T(8,128)}, f32[1,6,256,512]{2,1,3,0:T(8,128)}, f32[512,6,64]{0,2,1:T(8,128)}, bf16[4,1,256,384]{2,3,1,0:T(8...) while((s32[]{:T(128)}, f32[1,256,6,64]{1,3,2,0:T(8,128)}, ...), condition=%wide.region_14.18_spmd.clone, body=%wide.region_11.17_spmd.clone.sunk | while | flops 768058880 | bytes 276986912 | solution.py:238
  1611.9 66.6 %scatter_fusion = f32[6,256,512]{1,0,2:T(8,128)} fusion(f32[6,256,512]{1,0,2:T(8,128)} %bitcast.495, s32[511]{0:T(512)S(1)} %compare_select_fusion.6, f32[511,6,256]{2,1,0:T(8,128)} %copy.140), kind=kCustom, calls=%fused_computation.4.clone.clone.1 | custom fusion | flops 784896 | bytes 9420796 | tf_op jit(solution)/shard_map/while/body/eval_jaxpr/transpose(jvp(jit(_take)))/scatter-add | solution.py:33
  1713.7 66.6 %scatter_fusion.1 = f32[6,256,512]{1,0,2:T(8,128)} fusion(f32[6,256,512]{1,0,2:T(8,128)} %broadcast.448, s32[511]{0:T(512)S(1)} %compare_select_fusion.7, f32[511,6,256]{2,1,0:T(8,128)} %copy.142), kind=kCustom, calls=%fused_computation.5.clone.clone.1 | custom fusion | flops 784896 | bytes 9420796 | tf_op jit(solution)/shard_map/while/body/eval_jaxpr/transpose(jvp(jit(_take)))/scatter-add | solution.py:35
  1949.6 62.9 %scatter_fusion = f32[6,256,512]{1,0,2:T(8,128)} fusion(f32[6,256,512]{1,0,2:T(8,128)} %bitcast.495, s32[511]{0:T(512)S(1)} %compare_select_fusion.6, f32[511,6,256]{2,1,0:T(8,128)} %copy.140), kind=kCustom, calls=%fused_computation.4.clone.clone.1 | custom fusion | flops 784896 | bytes 9420796 | tf_op jit(solution)/shard_map/while/body/eval_jaxpr/transpose(jvp(jit(_take)))/scatter-add | solution.py:33
  2047.8 63.0 %scatter_fusion.1 = f32[6,256,512]{1,0,2:T(8,128)} fusion(f32[6,256,512]{1,0,2:T(8,128)} %broadcast.448, s32[511]{0:T(512)S(1)} %compare_select_fusion.7, f32[511,6,256]{2,1,0:T(8,128)} %copy.142), kind=kCustom, calls=%fused_computation.5.clone.clone.1 | custom fusion | flops 784896 | bytes 9420796 | tf_op jit(solution)/shard_map/while/body/eval_jaxpr/transpose(jvp(jit(_take)))/scatter-add | solution.py:35
  2280.2 66.6 %scatter_fusion = f32[6,256,512]{1,0,2:T(8,128)} fusion(f32[6,256,512]{1,0,2:T(8,128)} %bitcast.495, s32[511]{0:T(512)S(1)} %compare_select_fusion.6, f32[511,6,256]{2,1,0:T(8,128)} %copy.140), kind=kCustom, calls=%fused_computation.4.clone.clone.1 | custom fusion | flops 784896 | bytes 9420796 | tf_op jit(solution)/shard_map/while/body/eval_jaxpr/transpose(jvp(jit(_take)))/scatter-add | solution.py:33
  2382.0 66.7 %scatter_fusion.1 = f32[6,256,512]{1,0,2:T(8,128)} fusion(f32[6,256,512]{1,0,2:T(8,128)} %broadcast.448, s32[511]{0:T(512)S(1)} %compare_select_fusion.7, f32[511,6,256]{2,1,0:T(8,128)} %copy.142), kind=kCustom, calls=%fused_computation.5.clone.clone.1 | custom fusion | flops 784896 | bytes 9420796 | tf_op jit(solution)/shard_map/while/body/eval_jaxpr/transpose(jvp(jit(_take)))/scatter-add | solution.py:35
  2618.2 70.0 %scatter_fusion = f32[6,256,512]{1,0,2:T(8,128)} fusion(f32[6,256,512]{1,0,2:T(8,128)} %bitcast.495, s32[511]{0:T(512)S(1)} %compare_select_fusion.6, f32[511,6,256]{2,1,0:T(8,128)} %copy.140), kind=kCustom, calls=%fused_computation.4.clone.clone.1 | custom fusion | flops 784896 | bytes 9420796 | tf_op jit(solution)/shard_map/while/body/eval_jaxpr/transpose(jvp(jit(_take)))/scatter-add | solution.py:33
  2723.4 70.3 %scatter_fusion.1 = f32[6,256,512]{1,0,2:T(8,128)} fusion(f32[6,256,512]{1,0,2:T(8,128)} %broadcast.448, s32[511]{0:T(512)S(1)} %compare_select_fusion.7, f32[511,6,256]{2,1,0:T(8,128)} %copy.142), kind=kCustom, calls=%fused_computation.5.clone.clone.1 | custom fusion | flops 784896 | bytes 9420796 | tf_op jit(solution)/shard_map/while/body/eval_jaxpr/transpose(jvp(jit(_take)))/scatter-add | solution.py:35
  2923.7 137.8 %all-reduce.12.cloned.1.call-done = (f32[384,384]{0,1:T(8,128)}, f32[384,384]{0,1:T(8,128)}, f32[384,384]{0,1:T(8,128)}, f32[384,384]{1,0:T(8,128)}, f32[384,153...) async-done(((f32[384,384]{0,1:T(8,128)}, f32[384,384]{0,1:T(8,128)}, f32[384,384]{0,1:T(8,128)}, f32[384,384]{1,0:T(8,128)}, f32[384,1536]{1,0:T(8,128)}, ...) | async-done | bytes 7864336 | tf_op jit(solution)/shard_map/psum | solution.py:295
  (597 shorter events, 1367.3 us)
Async XLA Ops:
  7.2 1436.7 %copy-start = (bf16[384,1536]{1,0:T(8,128)(2,1)S(1)}, bf16[384,1536]{1,0:T(8,128)(2,1)}, u32[]{:S(2)}) copy-start(bf16[384,1536]{1,0:T(8,128)(2,1)} %param.40) | copy-start | bytes 3538948
  7.2 2848.4 %reduce-scatter.5.cloned.1.call-start = ((), (), s32[]{:S(2)}) async-start(), calls=%async_computation.3 | async-start | bytes 983040 | tf_op jit(solution)/shard_map/reduce_scatter | solution.py:244
  12.9 26.7 copy-start.6
  1278.1 10.2 copy-start.67
  1417.3 16.5 copy-start.19
  1441.8 19.9 copy-start.59
  1443.6 18.1 copy-start.13
  1443.7 18.1 copy-start.61
  1443.9 17.9 copy-start.63
  1451.3 7.6 copy-start.90
  1451.3 7.6 copy-start.91
  1467.6 7.5 copy-start.8
  1611.9 66.6 %copy-start.5 = (f32[1,6,256,256]{3,2,1,0:T(8,128)S(1)}, f32[1,6,256,256]{3,2,1,0:T(8,128)}, u32[]{:S(2)}) copy-start(f32[1,6,256,256]{3,2,1,0:T(8,128)} %get-tuple-element.726) | copy-start | bytes 4718596 | tf_op jit(solution)/shard_map/while
  1804.3 7.5 copy-start.8
  1949.6 62.9 %copy-start.5 = (f32[1,6,256,256]{3,2,1,0:T(8,128)S(1)}, f32[1,6,256,256]{3,2,1,0:T(8,128)}, u32[]{:S(2)}) copy-start(f32[1,6,256,256]{3,2,1,0:T(8,128)} %get-tuple-element.726) | copy-start | bytes 4718596 | tf_op jit(solution)/shard_map/while
  2135.0 7.5 copy-start.8
  2280.2 66.6 %copy-start.5 = (f32[1,6,256,256]{3,2,1,0:T(8,128)S(1)}, f32[1,6,256,256]{3,2,1,0:T(8,128)}, u32[]{:S(2)}) copy-start(f32[1,6,256,256]{3,2,1,0:T(8,128)} %get-tuple-element.726) | copy-start | bytes 4718596 | tf_op jit(solution)/shard_map/while
  2473.0 7.5 copy-start.8
  2618.2 70.0 %copy-start.5 = (f32[1,6,256,256]{3,2,1,0:T(8,128)S(1)}, f32[1,6,256,256]{3,2,1,0:T(8,128)}, u32[]{:S(2)}) copy-start(f32[1,6,256,256]{3,2,1,0:T(8,128)} %get-tuple-element.726) | copy-start | bytes 4718596 | tf_op jit(solution)/shard_map/while
  2825.0 51.8 %reduce-scatter.3.cloned.1.call-start = ((), (), s32[]{:S(2)}) async-start(), calls=%async_computation.2 | async-start | bytes 983040 | tf_op jit(solution)/shard_map/reduce_scatter | solution.py:241
  2825.7 235.9 %all-reduce.12.cloned.1.call-start = ((), (), s32[]{:S(2)}) async-start(), calls=%async_computation.4 | async-start | bytes 15728640 | tf_op jit(solution)/shard_map/psum | solution.py:295
  2878.8 43.8 %copy-start.29 = (f32[1,256,384]{2,1,0:T(8,128)S(1)}, f32[1,256,384]{2,1,0:T(8,128)}, u32[]{:S(2)}) copy-start(f32[1,256,384]{2,1,0:T(8,128)} %copy-done.28) | copy-start | bytes 1179652
  2878.9 43.8 %copy-start.43 = (bf16[384,384]{1,0:T(8,128)(2,1)S(1)}, bf16[384,384]{1,0:T(8,128)(2,1)}, u32[]{:S(2)}) copy-start(bf16[384,384]{1,0:T(8,128)(2,1)} %param.34) | copy-start | bytes 884740
  2878.9 43.8 %copy-start.66 = (f32[256]{0:T(256)S(1)}, f32[256]{0:T(256)}, u32[]{:S(2)}) copy-start(f32[256]{0:T(256)} %copy-done.65) | copy-start | bytes 3076
  (93 other events, 251.4 us)
Sparse Core Ops, SparseCore 0:
  2825.1 25.5 reduce-scatter.4
  2853.4 23.2 reduce-scatter.2
  2884.8 176.6 all-reduce.11
where the time goes:
time: 3120 us; the launch traced here: 3080 us
  local copies, waits for them, and re-layouts  2050 us (66%)
  other arithmetic  669 us (21%)
  waiting for transfers between devices  158 us (5%)
  matrix products  116 us (4%)
  blocking collectives  60.7 us (2%)
    unnamed x202, local copies, waits for them, and re-layouts  735 us
    slice x10, local copies, waits for them, and re-layouts, skewed(): flattened[..., row_count - 1:row_count - 1 + row_count * table_width]  523 us
    scatter-add x4, other arithmetic, band_terms(): jnp.take(key_table, key_index, axis=3)  266 us
    scatter-add x4, other arithmetic, band_terms(): jnp.take(query_table, query_index, axis=3)  266 us
    psum x1, waiting for transfers between devices, on_device(): lax.psum((g_query_weight, g_query_bias, g_key_weight, g_key_bias, g_value...  138 us
    reshape x17, local copies, waits for them, and re-layouts, skewed(): flattened.reshape(leading + (row_count, table_width))[..., :col_count]  131 us
    reshape x10, local copies, waits for them, and re-layouts, skewed(): flattened = padded.reshape(leading + (row_count * (table_width + 1),))  130 us
    pad x26, local copies, waits for them, and re-layouts, skewed(): jnp.pad(source_table, [(0, 0)] * (source_table.ndim - 1) + [(0, 1)])  120 us
  transfers between devices with their start and end apart: 3, of which 2 were waited for; matrix products, arithmetic and copies ran while one was open for 1% of the time, Pallas kernels for 0%

commit v1 on v0

v1 whole, which is shorter than its diff:
```python
import math

import jax
import jax.numpy as jnp
from jax import lax
from jax.experimental import pallas as pl
from jax.experimental.pallas import tpu as pltpu
from jax.sharding import PartitionSpec as P

HEADS = 6
BF = jnp.bfloat16
F32 = jnp.float32
LOG2E = math.log2(math.e)
EPS = 1e-07
VMEM_LIMIT = 56 * 1024 * 1024
EARLY_ROWS = 3584
LATE_ROWS = 1792


def nn(left, right):
    return lax.dot_general(left, right, (((1,), (0,)), ((), ())), preferred_element_type=F32)


def nt(left, right):
    return lax.dot_general(left, right, (((1,), (1,)), ((), ())), preferred_element_type=F32)


def tn(left, right):
    return lax.dot_general(left, right, (((0,), (0,)), ((), ())), preferred_element_type=F32)


def tt(left, right):
    return lax.dot_general(left, right, (((0,), (1,)), ((), ())), preferred_element_type=F32)


def lanes(shape):
    return lax.broadcasted_iota(jnp.int32, shape, len(shape) - 1)


def of_head(values, head):
    inside = (lanes(values.shape) // 64) == head
    return jnp.where(inside, values, jnp.zeros_like(values))


def pair_columns(pair):
    return pl.ds(pl.multiple_of(pair * 128, 128), 128)


def wide(column, width):
    return jnp.broadcast_to(column, (column.shape[0], width))


def reversal(size):
    rows = lax.broadcasted_iota(jnp.int32, (size, size), 0)
    cols = lax.broadcasted_iota(jnp.int32, (size, size), 1)
    return jnp.where(rows + cols == size - 1, 1.0, 0.0).astype(BF)


def place_blocks(block, x_all, own, core, far, diagonal):
    size = own.shape[0]
    even = block % 2 == 0
    core_at = jnp.where(even, 2 * size, 0)
    diagonal_at = jnp.where(even, 0, 2 * size)
    x_all[pl.ds(size, size), :] = own[...]
    x_all[pl.ds(3 * size, size), :] = far[...]
    x_all[pl.ds(pl.multiple_of(core_at, size), size), :] = core[...]
    x_all[pl.ds(pl.multiple_of(diagonal_at, size), size), :] = diagonal[...]


def position_terms(block, s_ref, own_rows, own_table, others, other_table, own_shift, other_shift):
    size = own_rows.shape[0]
    rel = own_table.shape[0]
    scores = nt(own_rows, own_table)
    last, first = scores[:, rel - 1 : rel], scores[:, 0:1]
    source = jnp.concatenate([scores, wide(last, size), wide(first, size)], axis=1)
    rolled = pltpu.roll(source, own_shift, 1, stride=1, stride_axis=0)
    for slot in range(3):
        rows = others(slot)
        if slot == 0:
            part = nt(rows, other_table[size:, :])
            part = jnp.concatenate([part, wide(part[:, size - 1 : size], size)], axis=1)
        elif slot == 1:
            part = nt(rows, other_table)
        else:
            part = nt(rows, other_table[:size, :])
            part = jnp.concatenate([wide(part[:, 0:1], size), part], axis=1)
        part = pltpu.roll(part, other_shift, 1, stride=1, stride_axis=0)[:, size:]
        span = slice(slot * size, (slot + 1) * size)
        s_ref[:, span] = rolled[:, span] + part.T
    low_half = block < 2
    constant = jnp.where(low_half, last, first)

    def constant_terms(slot):
        rows = others(slot)
        top = nt(other_table[0:16, :], rows)[0:1, :]
        bottom = nt(other_table[rel - 16 : rel, :], rows)[15:16, :]
        return constant + jnp.where(low_half, top, bottom)

    s_ref[:, 3 * size :] = constant_terms(3)

    @pl.when(block == 0)
    def _():
        s_ref[:, :size] = constant_terms(0)

    @pl.when(block == 3)
    def _():
        s_ref[:, 2 * size : 3 * size] = constant_terms(2)


def extend_table(block, ext_ref, table_ref):
    rel = table_ref.shape[0]
    half = rel // 2
    width = table_ref.shape[1]
    first, last = table_ref[0:1, :], table_ref[rel - 1 : rel, :]
    ext_ref[0:rel, :] = table_ref[...]
    ext_ref[rel : rel + half, :] = jnp.broadcast_to(last, (half, width))
    ext_ref[rel + half : 2 * rel, :] = jnp.broadcast_to(first, (half, width))
    far = jnp.where(block < 2, last.astype(F32), first.astype(F32)).astype(BF)
    ext_ref[2 * rel : 3 * rel, :] = jnp.broadcast_to(far, (rel, width))


def unskewed(block, wall_ref, near_ref, grad_rows, shift):
    size = grad_rows.shape[0]
    near_ref[:, : 3 * size] = grad_rows[:, : 3 * size]
    near_ref[:, 3 * size :] = jnp.zeros((size, size), BF)
    wall_ref[:, 4 * size : 5 * size] = grad_rows[:, 3 * size :]
    wall_ref[:, 5 * size :] = jnp.zeros((size, size), BF)

    @pl.when(block == 0)
    def _():
        wall_ref[:, 5 * size :] = near_ref[:, :size]
        near_ref[:, :size] = jnp.zeros((size, size), BF)

    @pl.when(block == 3)
    def _():
        wall_ref[:, 5 * size :] = near_ref[:, 2 * size : 3 * size]
        near_ref[:, 2 * size : 3 * size] = jnp.zeros((size, size), BF)

    wall_ref[:, : 4 * size] = pltpu.roll(near_ref[...], shift, 1, stride=1, stride_axis=0)


def table_grad(block, sums, scale):
    rel = sums.shape[1] // 3
    half = rel // 2
    over = jnp.sum(sums[:, rel : rel + half], axis=1, keepdims=True)
    under = jnp.sum(sums[:, rel + half : 2 * rel], axis=1, keepdims=True)
    far = jnp.sum(sums[:, 2 * rel :], axis=1, keepdims=True)
    over = over + jnp.where(block < 2, far, 0.0)
    under = under + jnp.where(block < 2, 0.0, far)
    at = lanes((sums.shape[0], rel))
    folded = sums[:, :rel] + jnp.where(at == rel - 1, over, 0.0) + jnp.where(at == 0, under, 0.0)
    return folded * scale


def affine(values, weight_ref, bias_ref):
    return nn(values, weight_ref[...]) + bias_ref[...].astype(F32)


def norm_forward(values):
    center = values - jnp.mean(values, axis=-1, keepdims=True)
    spread = jnp.mean(center * center, axis=-1, keepdims=True)
    rate = lax.rsqrt(spread + EPS)
    return center * rate, rate


def norm_backward(grad_hat, hat, rate):
    mean_grad = jnp.mean(grad_hat, axis=-1, keepdims=True)
    mean_along = jnp.mean(grad_hat * hat, axis=-1, keepdims=True)
    return rate * (grad_hat - mean_grad - hat * mean_along)


def column_sum(values):
    return jnp.sum(values.astype(F32), axis=0, keepdims=True)


def forward_kernel(
    block_ref, length_ref, own, core, far, diagonal,
    query_weight, query_bias, key_weight, key_bias, value_weight, value_bias,
    output_weight, output_bias, first_gain, first_bias, inner_weight, inner_bias,
    outer_weight, outer_bias, second_gain, second_bias, relative, relative_back, cotangent,
    layer_out, grad_first_out, chances_out, sent_out, query_out, key_out, value_out,
    rel_query_out, rel_key_out, grads_out,
    x_all, s_ref, mixture_ref, log_ref, active_ref, slope_ref,
):
    block = block_ref[0]
    length = length_ref[0]
    size, model_width = own.shape
    head_dim = model_width // HEADS
    factor = LOG2E / math.sqrt(3.0 * head_dim)
    place_blocks(block, x_all, own, core, far, diagonal)
    query_out[...] = affine(x_all[...], query_weight, query_bias).astype(BF)
    key_out[...] = affine(x_all[...], key_weight, key_bias).astype(BF)
    value_out[...] = affine(x_all[...], value_weight, value_bias).astype(BF)
    rel_query_out[...] = affine(relative[...], query_weight, query_bias).astype(BF)
    rel_key_out[...] = affine(relative_back[...], key_weight, key_bias).astype(BF)
    step = lanes((1, 4 * size))
    position = ((block + 3 + step // size) % 4) * size + step % size
    mask_row = jnp.where(position < length, 0.0, -1e30)
    stat_lane = lanes((size, 128))
    log_ref[...] = jnp.zeros_like(log_ref)

    def pair_step(pair, carry):
        columns = pair_columns(pair)
        total = jnp.zeros((size, 128), F32)
        for side in range(2):
            head = 2 * pair + side
            query_own = of_head(query_out[size : 2 * size, columns], side)
            position_terms(
                block,
                s_ref,
                query_own,
                rel_key_out[:, columns],
                lambda slot: key_out[slot * size : (slot + 1) * size, columns],
                of_head(rel_query_out[:, columns], side),
                1,
                0,
            )
            content = nt(query_own, key_out[:, columns])
            s_ref[...] = (s_ref[...] + content) * factor + mask_row
            top = jnp.max(s_ref[...], axis=1, keepdims=True)
            raised = jnp.exp2(s_ref[...] - top)
            s_ref[...] = raised
            row_sum = jnp.sum(raised, axis=1, keepdims=True)
            chances = (s_ref[...] * (1.0 / row_sum)).astype(BF)
            chances_out[head] = chances
            log_total = top + jnp.log2(row_sum)
            log_ref[...] = jnp.where(stat_lane % 8 == head, log_total, log_ref[...])
            total = total + nn(chances, of_head(value_out[:, columns], side))
        mixture_ref[:, columns] = total
        return carry

    lax.fori_loop(0, HEADS // 2, pair_step, 0)

    inner_width = inner_weight.shape[1]
    chunks = inner_width // model_width
    mixture_low = mixture_ref[...].astype(BF)
    first_sum = own[...].astype(F32) + affine(mixture_low, output_weight, output_bias)
    first_hat, first_rate = norm_forward(first_sum)
    normed = (first_hat * first_gain[...].astype(F32) + first_bias[...].astype(F32)).astype(BF)
    root_half = math.sqrt(0.5)
    density = 1.0 / math.sqrt(2.0 * math.pi)

    second_sum = normed.astype(F32) + outer_bias[...].astype(F32)
    for chunk in range(chunks):
        span = slice(chunk * model_width, (chunk + 1) * model_width)
        inner_pre = nn(normed, inner_weight[:, span]) + inner_bias[:, span].astype(F32)
        below = 0.5 + 0.5 * lax.erf(inner_pre * root_half)
        slope_ref[:, span] = below + inner_pre * density * jnp.exp(-0.5 * inner_pre * inner_pre)
        active_ref[:, span] = (inner_pre * below).astype(BF)
        second_sum = second_sum + nn(active_ref[:, span], outer_weight[span, :])
    second_hat, second_rate = norm_forward(second_sum)
    gain = second_gain[...].astype(F32)
    layer_out[...] = second_hat * gain + second_bias[...].astype(F32)
    cot = cotangent[...].astype(F32)
    grad_second = norm_backward(cot * gain, second_hat, second_rate)
    grad_outer = grad_second.astype(BF)
    outer_at, inner_at, output_at, small_at = 0, inner_width, 2 * inner_width, 2 * inner_width + model_width
    grads_out[small_at:, :] = jnp.zeros((grads_out.shape[0] - small_at, model_width), BF)
    small = [column_sum(grad_outer), column_sum(cot * second_hat), column_sum(cot)]
    grad_normed = grad_second
    for chunk in range(chunks):
        span = slice(chunk * model_width, (chunk + 1) * model_width)
        grads_out[outer_at + chunk * model_width : outer_at + (chunk + 1) * model_width, :] = tn(
            active_ref[:, span], grad_outer
        ).astype(BF)
        grad_inner = (nt(grad_outer, outer_weight[span, :]) * slope_ref[:, span]).astype(BF)
        small.append(column_sum(grad_inner))
        grads_out[inner_at + chunk * model_width : inner_at + (chunk + 1) * model_width, :] = tn(
            normed, grad_inner
        ).astype(BF)
        grad_normed = grad_normed + nt(grad_inner, inner_weight[:, span])
    grad_normed = grad_normed.astype(BF).astype(F32)
    grad_first = norm_backward(grad_normed * first_gain[...].astype(F32), first_hat, first_rate)
    grad_first_out[...] = grad_first
    grad_branch = grad_first.astype(BF)
    grads_out[output_at : output_at + model_width, :] = tn(mixture_low, grad_branch).astype(BF)
    small += [column_sum(grad_normed * first_hat), column_sum(grad_normed), column_sum(grad_branch)]
    small += [jnp.zeros((16 - len(small), model_width), F32)]
    grads_out[small_at : small_at + 16, :] = jnp.concatenate(small, axis=0).astype(BF)
    grad_mixture = nt(grad_branch, output_weight[...]).astype(BF)
    sent_out[:, :model_width] = grad_mixture
    along = grad_mixture.astype(F32) * mixture_ref[...]
    stats = jnp.where(stat_lane < 16, 0.0, log_ref[...])
    for head in range(HEADS):
        columns = slice((head // 2) * 128, (head // 2 + 1) * 128)
        delta = jnp.sum(of_head(along[:, columns], head % 2), axis=1, keepdims=True)
        stats = jnp.where((stat_lane == head) | (stat_lane == 8 + head), delta, stats)
    upper = stats.astype(BF).astype(F32)
    rest = stats - upper
    middle = rest.astype(BF).astype(F32)
    group = stat_lane // 8
    parts = jnp.where((group == 0) | (group == 2), upper, jnp.where((group == 1) | (group == 3), middle, rest - middle))
    sent_out[:, model_width:] = jnp.where(group < 5, parts, 0.0).astype(BF)


def position_backward(block, side, grad_scores, flip, other_pair, ext_pair, own_rows_back, wall_ref, near_ref, shift):
    grad_back = nn(flip, grad_scores).astype(BF)
    unskewed(block, wall_ref, near_ref, grad_back, shift)
    row_grad = nn(grad_back, of_head(other_pair, side)) + nn(wall_ref[...], of_head(ext_pair, side))
    return row_grad, tn(of_head(own_rows_back, side), wall_ref[...])


def query_kernel(
    block_ref, chances, sent, query_all, key_all, value_all, rel_key,
    grad_query_out, grad_rel_key_out,
    ext_ref, wall_ref, near_ref, back_ref, sum_ref, rows_ref,
):
    block = block_ref[0]
    size, model_width = grad_query_out.shape
    scale = 1.0 / math.sqrt(3.0 * (model_width // HEADS))
    flip = reversal(size)
    extend_table(block, ext_ref, rel_key)
    back_ref[...] = nn(flip, query_all[size : 2 * size, :]).astype(BF)
    stats = sent[:, model_width:].astype(F32)
    stat_lane = lanes((size, 128))

    def pair_step(pair, carry):
        columns = pair_columns(pair)
        row_grad = jnp.zeros((size, 128), F32)
        for side in range(2):
            head = 2 * pair + side
            delta = jnp.sum(
                jnp.where((stat_lane == head) | (stat_lane == 8 + head), stats, 0.0), axis=1, keepdims=True
            )
            grad_mixture = of_head(sent[:, columns], side)
            grad_chances = nt(grad_mixture, value_all[:, columns])
            grad_scores = (chances[head].astype(F32) * (grad_chances - delta)).astype(BF)
            rows, table = position_backward(
                block, side, grad_scores, flip, key_all[:, columns], ext_ref[:, columns],
                back_ref[:, columns], wall_ref, near_ref, 3 * size,
            )
            row_grad = row_grad + rows
            if side == 0:
                sum_ref[...] = table
            else:
                sum_ref[...] += table
        rows_ref[:, columns] = (row_grad * scale).astype(BF)
        grad_rel_key_out[columns, :] = table_grad(block, sum_ref[...], scale)
        return carry

    lax.fori_loop(0, HEADS // 2, pair_step, 0)
    grad_query_out[...] = nn(flip, rows_ref[...]).astype(BF)


def key_kernel(
    block_ref, length_ref, own, sent_own, sent_core, sent_far, sent_diagonal, query_all, key_all, value_all,
    rel_query, rel_key, grad_query, grad_rel_key, grad_first,
    query_weight, key_weight, value_weight, relative,
    grad_tokens_out, grads_out,
    sent_ref, s_ref, grad_ref, ext_ref, wall_ref, near_ref, back_ref, sum_ref, key_rows_ref, value_rows_ref,
    rel_grad_ref, stat_ref,
):
    block = block_ref[0]
    length = length_ref[0]
    size, model_width = own.shape
    rel = rel_query.shape[0]
    scale = 1.0 / math.sqrt(3.0 * (model_width // HEADS))
    factor = LOG2E * scale
    flip = reversal(size)
    place_blocks(block, sent_ref, sent_own, sent_core, sent_far, sent_diagonal)
    extend_table(block, ext_ref, rel_query)
    back_ref[...] = nn(flip, key_all[size : 2 * size, :]).astype(BF)
    stats = sent_ref[:, model_width:].astype(F32).T
    stat_ref[0:8, :] = stats[0:8, :] + stats[8:16, :]
    stat_ref[8:16, :] = stats[16:24, :] + (stats[24:32, :] + stats[32:40, :])
    position = block * size + lax.broadcasted_iota(jnp.int32, (size, 1), 0)
    mask_column = jnp.where(position < length, 0.0, -1e30)

    def pair_step(pair, carry):
        columns = pair_columns(pair)
        row_grad = jnp.zeros((size, 128), F32)
        value_grad = jnp.zeros((size, 128), F32)
        for side in range(2):
            head = 2 * pair + side
            key_own = of_head(key_all[size : 2 * size, columns], side)
            position_terms(
                block,
                s_ref,
                key_own,
                rel_query[:, columns],
                lambda slot: query_all[slot * size : (slot + 1) * size, columns],
                of_head(rel_key[:, columns], side),
                0,
                1,
            )
            content = nt(key_own, query_all[:, columns])
            shift = mask_column - stat_ref[pl.ds(8 + head, 1), :]
            s_ref[...] = jnp.exp2((s_ref[...] + content) * factor + shift)
            value_grad = value_grad + nn(s_ref[...].astype(BF), of_head(sent_ref[:, columns], side))
            grad_chances = nt(of_head(value_all[size : 2 * size, columns], side), sent_ref[:, columns])
            grad_ref[...] = (s_ref[...] * (grad_chances - stat_ref[pl.ds(head, 1), :])).astype(BF)
            rows, table = position_backward(
                block, side, grad_ref[...], flip, query_all[:, columns], ext_ref[:, columns],
                back_ref[:, columns], wall_ref, near_ref, 3 * size + 1,
            )
            row_grad = row_grad + rows
            if side == 0:
                sum_ref[...] = table
            else:
                sum_ref[...] += table
        key_rows_ref[:, columns] = (row_grad * scale).astype(BF)
        value_rows_ref[:, columns] = value_grad.astype(BF)
        rel_grad_ref[columns, :] = table_grad(block, sum_ref[...], scale)
        return carry

    lax.fori_loop(0, HEADS // 2, pair_step, 0)
    grad_key = nn(flip, key_rows_ref[...]).astype(BF)
    grad_value = value_rows_ref[...]
    rel_query_grad = rel_grad_ref[...]
    rel_key_grad = grad_rel_key[...]
    query_low = rel_query_grad.astype(BF)
    key_low = nn(rel_key_grad.astype(BF), reversal(rel)).astype(BF)
    tokens = own[...]
    table = relative[...]
    grads_out[0:model_width, :] = (tn(tokens, grad_query[...]) + tt(table, query_low)).astype(BF)
    grads_out[model_width : 2 * model_width, :] = (tn(tokens, grad_key) + tt(table, key_low)).astype(BF)
    grads_out[2 * model_width : 3 * model_width, :] = tn(tokens, grad_value).astype(BF)
    table_at = 3 * model_width
    grads_out[table_at : table_at + rel, :] = (
        tt(query_low, query_weight[...]) + tt(key_low, key_weight[...])
    ).astype(BF)
    small_at = table_at + rel
    grads_out[small_at:, :] = jnp.zeros((grads_out.shape[0] - small_at, model_width), BF)
    ones = jnp.ones((8, rel), BF)

    def lane_sums(values):
        high = values.astype(BF)
        low = (values - high.astype(F32)).astype(BF)
        return (nt(ones, high) + nt(ones, low))[0:1, :]

    small = [
        column_sum(grad_query[...]) + lane_sums(rel_query_grad),
        column_sum(grad_key) + lane_sums(rel_key_grad),
        column_sum(grad_value),
        jnp.zeros((13, model_width), F32),
    ]
    grads_out[small_at : small_at + 16, :] = jnp.concatenate(small, axis=0).astype(BF)
    grad_tokens_out[...] = (
        nt(grad_query[...], query_weight[...])
        + nt(grad_key, key_weight[...])
        + nt(grad_value, value_weight[...])
        + grad_first[...]
    )


def call(kernel, outs, scratch, *operands, scalars):
    in_specs = [pl.BlockSpec(memory_space=pltpu.SMEM)] * scalars
    in_specs += [pl.BlockSpec(memory_space=pltpu.VMEM)] * (len(operands) - scalars)
    return pl.pallas_call(
        kernel,
        out_shape=[jax.ShapeDtypeStruct(shape, kind) for shape, kind in outs],
        in_specs=in_specs,
        out_specs=[pl.BlockSpec(memory_space=pltpu.VMEM)] * len(outs),
        scratch_shapes=[pltpu.VMEM(shape, kind) for shape, kind in scratch],
        compiler_params=pltpu.CompilerParams(vmem_limit_bytes=VMEM_LIMIT),
    )(*operands)


def hop_table(blk_count, dp_count, bit_of):
    pairs = []
    for blk in range(blk_count):
        for dp in range(dp_count):
            axis, bit = bit_of(blk)
            there = (blk ^ bit, dp) if axis == 0 else (blk, dp ^ bit)
            pairs.append((blk * dp_count + dp, there[0] * dp_count + there[1]))
    return pairs


def all_sum(early, late, blk_count, dp_count):
    both = ("blk", "dp")
    blk, dp = lax.axis_index("blk"), lax.axis_index("dp")
    steps = [lambda b: (0, 1)]
    first, second = (0, 2), (1, 1)
    steps.append(lambda b: first if b % 2 == 0 else second)
    steps.append(lambda b: second if b % 2 == 0 else first)
    bit = 2
    while bit < dp_count:
        steps.append(lambda b, bit=bit: (1, bit))
        bit *= 2

    def my_bit(step):
        axis0, bit0 = step(0)
        axis1, bit1 = step(1)
        even = (blk if axis0 == 0 else dp) // bit0 % 2
        odd = (blk if axis1 == 0 else dp) // bit1 % 2
        return jnp.where(blk % 2 == 0, even, odd)

    def exchange(values, step):
        return lax.ppermute(values, both, hop_table(blk_count, dp_count, step))

    bit = my_bit(steps[0])

    def half(values, which):
        rows = values.shape[0] // 2
        return lax.dynamic_slice_in_dim(values, which * rows, rows, 0)

    early_in = exchange(half(early, 1 - bit), steps[0])
    late_in = exchange(half(late, 1 - bit), steps[0])
    mine = jnp.concatenate(
        [
            half(early, bit).astype(F32) + early_in.astype(F32),
            half(late, bit).astype(F32) + late_in.astype(F32),
        ],
        axis=0,
    )
    terms = [mine.astype(BF)]
    for step in steps[1:]:
        bit = my_bit(step)
        send = sum(half(t, 1 - bit).astype(F32) for t in terms).astype(BF)
        arrived = exchange(send, step)
        terms = [half(t, bit) for t in terms] + [arrived]
    held = sum(t.astype(F32) for t in terms).astype(BF)
    for step in reversed(steps[1:]):
        bit = my_bit(step)
        arrived = exchange(held, step)
        rows = held.shape[0]
        held = jnp.where(
            bit == 0, jnp.concatenate([held, arrived], axis=0), jnp.concatenate([arrived, held], axis=0)
        )
    bit = my_bit(steps[0])
    arrived = exchange(held, steps[0])
    low = jnp.where(bit == 0, held, arrived)
    high = jnp.where(bit == 0, arrived, held)
    cut = early.shape[0] // 2
    return (
        jnp.concatenate([low[:cut], high[:cut]], axis=0).astype(F32),
        jnp.concatenate([low[cut:], high[cut:]], axis=0).astype(F32),
    )


def on_device(
    blk_count, dp_count,
    tokens, lengths, query_weight, query_bias, key_weight, key_bias, value_weight, value_bias,
    output_weight, output_bias, first_gain, first_bias, inner_weight, inner_bias, outer_weight, outer_bias,
    second_gain, second_bias, relative_table, cotangent,
):
    seq_count, size, width = tokens.shape
    rel = relative_table.shape[0]
    inner_width = inner_weight.shape[1]
    own = tokens[0]
    block = lax.axis_index("blk").astype(jnp.int32).reshape(1)

    def along(values, bit):
        return lax.ppermute(values, "blk", [(i, i ^ bit) for i in range(blk_count)])

    def row(vector):
        return vector.reshape(1, -1)

    far = along(own, 2)
    core = along(own, 1)
    diagonal = along(far, 1)
    relative_back = jnp.flip(relative_table, 0)
    full = blk_count * size
    (
        layer_out, grad_first, chances, sent, query_all, key_all, value_all, rel_query, rel_key, early,
    ) = call(
        forward_kernel,
        [
            ((size, width), F32),
            ((size, width), F32),
            ((HEADS, size, full), BF),
            ((size, width + 128), BF),
            ((full, width), BF),
            ((full, width), BF),
            ((full, width), BF),
            ((rel, width), BF),
            ((rel, width), BF),
            ((EARLY_ROWS, width), BF),
        ],
        [
            ((full, width), BF),
            ((size, full), F32),
            ((size, width), F32),
            ((size, 128), F32),
            ((size, inner_width), BF),
            ((size, inner_width), F32),
        ],
        block, lengths, own, core, far, diagonal,
        query_weight, row(query_bias), key_weight, row(key_bias), value_weight, row(value_bias),
        output_weight, row(output_bias), row(first_gain), row(first_bias), inner_weight, row(inner_bias),
        outer_weight, row(outer_bias), row(second_gain), row(second_bias), relative_table, relative_back,
        cotangent[0],
        scalars=2,
    )
    sent_far = along(sent, 2)
    sent_core = along(sent, 1)
    sent_diagonal = along(sent, 3)
    shared_scratch = [
        ((3 * rel, width), BF),
        ((size, 3 * rel), BF),
        ((size, full), BF),
        ((size, width), BF),
        ((128, 3 * rel), F32),
        ((size, width), BF),
    ]
    grad_query, grad_rel_key = call(
        query_kernel,
        [((size, width), BF), ((width, rel), F32)],
        shared_scratch,
        block, chances, sent, query_all, key_all, value_all, rel_key,
        scalars=1,
    )
    grad_tokens, late = call(
        key_kernel,
        [((size, width), F32), ((LATE_ROWS, width), BF)],
        [((full, width + 128), BF), ((size, full), F32), ((size, full), BF)]
        + shared_scratch
        + [((size, width), BF), ((width, rel), F32), ((16, full), F32)],
        block, lengths, own, sent, sent_core, sent_far, sent_diagonal, query_all, key_all, value_all,
        rel_query, rel_key, grad_query, grad_rel_key, grad_first,
        query_weight, key_weight, value_weight, relative_table,
        scalars=2,
    )
    early, late = all_sum(early, late, blk_count, dp_count)
    inner_at, output_at = inner_width, 2 * inner_width
    small_at = output_at + width
    small = early[small_at : small_at + 16]
    late_at = 3 * width + rel
    late_small = late[late_at : late_at + 16]
    g_inner_weight = jnp.concatenate(
        [early[inner_at + k * width : inner_at + (k + 1) * width] for k in range(inner_width // width)], axis=1
    )
    chunks = inner_width // width
    return (
        layer_out[None],
        grad_tokens[None],
        late[0:width],
        late_small[0],
        late[width : 2 * width],
        late_small[1],
        late[2 * width : 3 * width],
        late_small[2],
        early[output_at : output_at + width],
        small[5 + chunks],
        small[3 + chunks],
        small[4 + chunks],
        g_inner_weight,
        small[3 : 3 + chunks].reshape(-1),
        early[0:inner_width],
        small[0],
        small[1],
        small[2],
        late[3 * width : 3 * width + rel],
    )


def solution(mesh):
    blk_count, dp_count = mesh.shape["blk"], mesh.shape["dp"]
    rows = P("dp", "blk", None)
    in_specs = (rows, P("dp")) + (P(),) * 17 + (rows,)
    out_specs = (rows, rows) + (P(),) * 17

    def whole(*arrays):
        return on_device(blk_count, dp_count, *arrays)

    return jax.shard_map(whole, mesh=mesh, in_specs=in_specs, out_specs=out_specs, check_vma=False)
```

time: 3120 us -> 207 us (0.07); the launches traced: 3080 us -> 206 us
  local copies, waits for them, and re-layouts: 2050 us -> 27.9 us
  other arithmetic: 669 us -> 15.3 us
  matrix products: 116 us -> 0 us
  waiting for transfers between devices: 158 us -> 69.2 us
  Pallas kernels: 0 us -> 61.1 us
  blocking collectives: 60.7 us -> 0 us
    unnamed x202 -> x10, local copies, waits for them, and re-layouts: 735 us -> 1.37 us
    scatter-add x8 -> x0, other arithmetic: 533 us -> none  [the longest x4 266 us: band_terms(): jnp.take(key_table, key_index, axis=3)]
    slice x19 -> x7, local copies, waits for them, and re-layouts: 535 us -> 4.43 us  [the longest x1 1.56 us: on_device(): early[0:inner_width]]
    reshape x27 -> x11, local copies, waits for them, and re-layouts: 261 us -> 13.1 us  [the longest x10 12.5 us: row(): return vector.reshape(1, -1)]
    pad x42 -> x0, local copies, waits for them, and re-layouts: 229 us -> none  [the longest x26 120 us: skewed(): jnp.pad(source_table, [(0, 0)] * (source_table.ndim - 1) + [(0, 1)])]
    psum x1 -> x0, waiting for transfers between devices: 138 us -> none  [on_device(): lax.psum((g_query_weight, g_query_bias, g_key_weight, g_key_bias, g_value...]
    dot_general x76 -> x0, matrix products: 116 us -> none  [the longest x14 20.1 us: split_einsum(): jnp.einsum(formula, lower_part, narrow_values, preferred_element_type=jnp...]
    gather x10 -> x0, local copies, waits for them, and re-layouts: 94.2 us -> none  [the longest x5 63.5 us: band_terms(): jnp.take(key_table, key_index, axis=3)]
  transfers between devices with their start and end apart: 3 -> 17, of which waited for: 2 -> 12; matrix products, arithmetic and copies ran while one was open for 1% -> 10% of each run, Pallas kernels for 0% -> 17%
where the time goes in v1:
time: 207 us; the launch traced here: 206 us
  waiting for transfers between devices  69.2 us (33%)
  Pallas kernels  61.1 us (30%)
  starting transfers between devices  31 us (15%)
  local copies, waits for them, and re-layouts  27.9 us (13%)
  other arithmetic  15.3 us (7%)
    ppermute x11, waiting for transfers between devices, exchange(): return lax.ppermute(values, both, hop_table(blk_count, dp_count, step))  65.4 us
    pallas_call x3, Pallas kernels, call(): pl.pallas_call(kernel, out_shape=[jax.ShapeDtypeStruct(shape, kind) for s...  61.1 us
    ppermute x11, starting transfers between devices, exchange(): return lax.ppermute(values, both, hop_table(blk_count, dp_count, step))  25 us
    reshape x10, local copies, waits for them, and re-layouts, row(): return vector.reshape(1, -1)  12.5 us
    rev x1, local copies, waits for them, and re-layouts, on_device(): relative_back = jnp.flip(relative_table, 0)  6.34 us
    ppermute x6, starting transfers between devices, along(): return lax.ppermute(values, 'blk', [(i, i ^ bit) for i in range(blk_count)])  5.96 us
    convert_element_type x3, other arithmetic, all_sum(): send = sum((half(t, 1 - bit).astype(F32) for t in terms)).astype(BF)  4.86 us
  transfers between devices with their start and end apart: 17, of which 12 were waited for; matrix products, arithmetic and copies ran while one was open for 10% of the time, Pallas kernels for 17%

profile of v1, /device:TPU:9, one launch (start us, length us, event | category | flops | bytes accessed | tf_op | source)
XLA Modules:
  0.0 206.1 jit_solution(14408478317506627681)
XLA Ops:
  2.9 3.8 %collective-permute-done.1.far = bf16[256,384]{1,0:T(8,128)(2,1)S(1)} collective-permute-done((bf16[256,384]{1,0:T(8,128)(2,1)}, bf16[256,384]{1,0:T(8,128)(2,1)S(1)}, u32[]{:S(2)}, u32[]{:S(2)}) %collective-permute-start.1) | collective-permute-done | bytes 196640 | tf_op jit(solution)/shard_map/ppermute | solution.py:544
  21.4 6.3 %rev.4.relative_back = bf16[512,384]{1,0:T(8,128)(2,1)} reverse(bf16[512,384]{1,0:T(8,128)(2,1)} %relative.3), dimensions={0} | reverse | bytes 786432 | tf_op jit(solution)/shard_map/jit(_flip)/rev | solution.py:552
  28.5 25.8 %shard_map.339 = (f32[256,384]{1,0:T(8,128)}, f32[256,384]{1,0:T(8,128)}, bf16[6,256,1024]{2,1,0:T(8,128)(2,1)}, bf16[256,512]{1,0:T(8,128)(2,1)}, bf16[1024,384...) custom-call(s32[1]{0:T(128)} %bitcast.block_ref, ...), custom_call_target="tpu_custom_call" | custom-call | tf_op jit(solution)/shard_map/pallas_call | solution.py:449
  57.0 1.7 collective-permute-start.5
  59.1 11.2 %shard_map.340 = (bf16[256,384]{1,0:T(8,128)(2,1)}, f32[384,512]{1,0:T(8,128)}) custom-call(s32[1]{0:T(128)} %bitcast.block_ref, bf16[6,256,1024]{2,1,0:T(8,128)(2,1)} %get-tuple-element.40.chances, bf16[256,512]{1,0:T(8,128)(2,1)} %get-tuple-element.34.sent.sent_own, bf16[1024,384]{1,0:T(8,128)(2,1)} %get-tuple-element.35.query_all, ...), custom_call_target="tpu_custom_call" | custom-call | tf_op jit(solution)/shard_map/pallas_call | solution.py:449
  71.0 24.1 %shard_map.341 = (f32[256,384]{1,0:T(8,128)}, bf16[1792,384]{1,0:T(8,128)(2,1)}) custom-call(s32[1]{0:T(128)} %bitcast.block_ref, s32[1]{0:T(128)S(6)} %copy.39.length_ref, bf16[256,384]{1,0:T(8,128)(2,1)} %bitcast.8, bf16[256,512]{1,0:T(8,128)(2,1)} %get-tuple-element.34.sent.sent_own, bf16[256,512]{1,0:T(8,128)(2,1)} %collective-permute-done.3.sent_core, ...), custom_call_target="tpu_custom_call" | custom-call | tf_op jit(solution)/shard_map/pallas_call | solution.py:449
  98.0 1.9 collective-permute-done.7
  101.4 1.7 add_convert_fusion
  103.1 1.8 fusion
  106.1 12.7 %collective-permute-done.8 = bf16[1344,384]{1,0:T(8,128)(2,1)} collective-permute-done((bf16[1344,384]{1,0:T(8,128)(2,1)S(1)}, bf16[1344,384]{1,0:T(8,128)(2,1)}, u32[]{:S(2)}, u32[]{:S(2)}) %collective-permute-start.8) | collective-permute-done | bytes 1032224 | tf_op jit(solution)/shard_map/ppermute | solution.py:489
  118.8 2.2 %add_convert_fusion.2 = bf16[672,384]{1,0:T(8,128)(2,1)S(1)} fusion(s32[]{:T(128)S(6)} %dynamic_slice.114, bf16[1792,384]{1,0:T(8,128)(2,1)S(1)} %add_convert_fusion, bf16[896,384]{1,0:T(8,128)(2,1)S(1)} %add_convert_fusion.1, bf16[1344,384]{1,0:T(8,128)(2,1)} %collective-permute-done.8, s32[]{:T(128)S(6)} %select_n.246), kind=kLoop, calls=%fused_computation.20 | loop fusion | flops 1806336 | bytes 3096584 | tf_op jit(solution)/shard_map/convert_element_type | solution.py:509
  122.5 6.8 %collective-permute-done.9 = bf16[672,384]{1,0:T(8,128)(2,1)S(1)} collective-permute-done((bf16[672,384]{1,0:T(8,128)(2,1)S(1)}, bf16[672,384]{1,0:T(8,128)(2,1)S(1)}, u32[]{:S(2)}, u32[]{:S(2)}) %collective-permute-start.9) | collective-permute-done | bytes 516128 | tf_op jit(solution)/shard_map/ppermute | solution.py:489
  131.0 5.5 %collective-permute-done.10 = bf16[336,384]{1,0:T(8,128)(2,1)S(1)} collective-permute-done((bf16[336,384]{1,0:T(8,128)(2,1)S(1)}, bf16[336,384]{1,0:T(8,128)(2,1)S(1)}, u32[]{:S(2)}, u32[]{:S(2)}) %collective-permute-start.10) | collective-permute-done | bytes 258080 | tf_op jit(solution)/shard_map/ppermute | solution.py:489
  137.6 2.4 %collective-permute-start.11 = (bf16[168,384]{1,0:T(8,128)(2,1)S(1)}, bf16[168,384]{1,0:T(8,128)(2,1)S(1)}, u32[]{:S(2)}, u32[]{:S(2)}) collective-permute-start(bf16[168,384]{1,0:T(8,128)(2,1)S(1)} %add_convert_fusion.5), channel_id=1, source_target_pairs={{0,4},{1,5},{2,6},{3,7},{4,0},{5,1},{6,2},{7,3},{8,12},{9,13},{10,... | collective-permute-start | bytes 387080 | tf_op jit(solution)/shard_map/ppermute | solution.py:489
  140.0 3.2 %collective-permute-done.11 = bf16[168,384]{1,0:T(8,128)(2,1)S(1)} collective-permute-done((bf16[168,384]{1,0:T(8,128)(2,1)S(1)}, bf16[168,384]{1,0:T(8,128)(2,1)S(1)}, u32[]{:S(2)}, u32[]{:S(2)}) %collective-permute-start.11) | collective-permute-done | bytes 129056 | tf_op jit(solution)/shard_map/ppermute | solution.py:489
  144.4 2.9 %collective-permute-start.12 = (bf16[168,384]{1,0:T(8,128)(2,1)S(1)}, bf16[168,384]{1,0:T(8,128)(2,1)S(1)}, u32[]{:S(2)}, u32[]{:S(2)}) collective-permute-start(bf16[168,384]{1,0:T(8,128)(2,1)S(1)} %add_convert_fusion.4), channel_id=1, source_target_pairs={{0,4},{1,5},{2,6},{3,7},{4,0},{5,1},{6,2},{7,3},{8,12},{9,13},{10,... | collective-permute-start | bytes 387080 | tf_op jit(solution)/shard_map/ppermute | solution.py:489
  147.2 2.4 %collective-permute-done.12 = bf16[168,384]{1,0:T(8,128)(2,1)S(1)} collective-permute-done((bf16[168,384]{1,0:T(8,128)(2,1)S(1)}, bf16[168,384]{1,0:T(8,128)(2,1)S(1)}, u32[]{:S(2)}, u32[]{:S(2)}) %collective-permute-start.12) | collective-permute-done | bytes 129056 | tf_op jit(solution)/shard_map/ppermute | solution.py:489
  149.8 1.8 collective-permute-start.13
  151.5 4.7 %collective-permute-done.13 = bf16[336,384]{1,0:T(8,128)(2,1)S(1)} collective-permute-done((bf16[336,384]{1,0:T(8,128)(2,1)S(1)}, bf16[336,384]{1,0:T(8,128)(2,1)S(1)}, u32[]{:S(2)}, u32[]{:S(2)}) %collective-permute-start.13) | collective-permute-done | bytes 258080 | tf_op jit(solution)/shard_map/ppermute | solution.py:489
  157.6 6.8 %collective-permute-done.14 = bf16[672,384]{1,0:T(8,128)(2,1)S(1)} collective-permute-done((bf16[672,384]{1,0:T(8,128)(2,1)S(1)}, bf16[672,384]{1,0:T(8,128)(2,1)S(1)}, u32[]{:S(2)}, u32[]{:S(2)}) %collective-permute-start.14) | collective-permute-done | bytes 516128 | tf_op jit(solution)/shard_map/ppermute | solution.py:489
  166.1 17.7 %collective-permute-done.15 = bf16[1344,384]{1,0:T(8,128)(2,1)S(1)} collective-permute-done((bf16[1344,384]{1,0:T(8,128)(2,1)S(1)}, bf16[1344,384]{1,0:T(8,128)(2,1)S(1)}, u32[]{:S(2)}, u32[]{:S(2)}) %collective-permute-start.15) | collective-permute-done | bytes 1032224 | tf_op jit(solution)/shard_map/ppermute | solution.py:489
  184.3 9.7 %collective-permute-start.16 = (bf16[2688,384]{1,0:T(8,128)(2,1)S(1)}, bf16[2688,384]{1,0:T(8,128)(2,1)S(1)}, u32[]{:S(2)}, u32[]{:S(2)}) collective-permute-start(bf16[2688,384]{1,0:T(8,128)(2,1)S(1)} %maximum_select_fusion), channel_id=1, source_target_pairs={{0,8},{1,9},{2,10},{3,11},{4,12},{5,13},{6,14},{7,15},{8,0},{9,1},... | collective-permute-start | bytes 6193160 | tf_op jit(solution)/shard_map/ppermute | solution.py:489
  194.0 3.7 %collective-permute-done.16 = bf16[2688,384]{1,0:T(8,128)(2,1)S(1)} collective-permute-done((bf16[2688,384]{1,0:T(8,128)(2,1)S(1)}, bf16[2688,384]{1,0:T(8,128)(2,1)S(1)}, u32[]{:S(2)}, u32[]{:S(2)}) %collective-permute-start.16) | collective-permute-done | bytes 2064416 | tf_op jit(solution)/shard_map/ppermute | solution.py:489
  204.4 1.7 pad_maximum_fusion
  (61 shorter events, 42.3 us)
Async XLA Ops:
  0.7 6.0 %collective-permute-start.1 = (bf16[256,384]{1,0:T(8,128)(2,1)}, bf16[256,384]{1,0:T(8,128)(2,1)S(1)}, u32[]{:S(2)}, u32[]{:S(2)}) collective-permute-start(bf16[256,384]{1,0:T(8,128)(2,1)} %bitcast.5), channel_id=1, source_target_pairs={{0,16},{8,24},{16,0},{24,8},{1,17},{9,25},{17,1},{25,9},{2,18},{10... | collective-permute-start | bytes 589832 | tf_op jit(solution)/shard_map/ppermute | solution.py:544
  2.0 25.8 %collective-permute-start = (bf16[256,384]{1,0:T(8,128)(2,1)}, bf16[256,384]{1,0:T(8,128)(2,1)S(1)}, u32[]{:S(2)}, u32[]{:S(2)}) collective-permute-start(bf16[256,384]{1,0:T(8,128)(2,1)} %bitcast.6), channel_id=1, source_target_pairs={{0,8},{8,0},{16,24},{24,16},{1,9},{9,1},{17,25},{25,17},{2,10},{10... | collective-permute-start | bytes 589832 | tf_op jit(solution)/shard_map/ppermute | solution.py:544
  6.7 21.0 %copy-start.2 = (bf16[256,384]{1,0:T(8,128)(2,1)}, bf16[256,384]{1,0:T(8,128)(2,1)S(1)}, u32[]{:S(2)}) copy-start(bf16[256,384]{1,0:T(8,128)(2,1)S(1)} %collective-permute-done.1.far) | copy-start | bytes 589828
  6.7 21.0 %collective-permute-start.2 = (bf16[256,384]{1,0:T(8,128)(2,1)S(1)}, bf16[256,384]{1,0:T(8,128)(2,1)S(1)}, u32[]{:S(2)}, u32[]{:S(2)}) collective-permute-start(bf16[256,384]{1,0:T(8,128)(2,1)S(1)} %collective-permute-done.1.far), channel_id=1, source_target_pairs={{0,8},{8,0},{16,24},{24,16},{1,9},{9,1},{17,25},{25,17},{2,10},{10... | collective-permute-start | bytes 589832 | tf_op jit(solution)/shard_map/ppermute | solution.py:544
  27.7 0.7 copy-start.3
  27.7 0.8 copy-start.4
  54.3 2.7 %copy-start = (bf16[256,512]{1,0:T(8,128)(2,1)S(1)}, bf16[256,512]{1,0:T(8,128)(2,1)}, u32[]{:S(2)}) copy-start(bf16[256,512]{1,0:T(8,128)(2,1)} %get-tuple-element.34.sent.sent_own) | copy-start | bytes 786436
  55.8 45.6 %collective-permute-start.6 = (bf16[1792,384]{1,0:T(8,128)(2,1)S(1)}, bf16[1792,384]{1,0:T(8,128)(2,1)S(1)}, u32[]{:S(2)}, u32[]{:S(2)}) collective-permute-start(bf16[1792,384]{1,0:T(8,128)(2,1)S(1)} %constant_dynamic-slice_fusion.1), channel_id=1, source_target_pairs={{0,8},{1,9},{2,10},{3,11},{4,12},{5,13},{6,14},{7,15},{8,0},{9,1},... | collective-permute-start | bytes 4128776 | tf_op jit(solution)/shard_map/ppermute | solution.py:489
  57.0 13.4 %collective-permute-start.5 = (bf16[256,512]{1,0:T(8,128)(2,1)S(1)}, bf16[256,512]{1,0:T(8,128)(2,1)S(1)}, u32[]{:S(2)}, u32[]{:S(2)}) collective-permute-start(bf16[256,512]{1,0:T(8,128)(2,1)S(1)} %copy-done), channel_id=1, source_target_pairs={{0,24},{8,16},{16,8},{24,0},{1,25},{9,17},{17,9},{25,1},{2,26},{10... | collective-permute-start | bytes 786440 | tf_op jit(solution)/shard_map/ppermute | solution.py:544
  58.6 11.8 %collective-permute-start.4 = (bf16[256,512]{1,0:T(8,128)(2,1)S(1)}, bf16[256,512]{1,0:T(8,128)(2,1)}, u32[]{:S(2)}, u32[]{:S(2)}) collective-permute-start(bf16[256,512]{1,0:T(8,128)(2,1)S(1)} %copy-done), channel_id=1, source_target_pairs={{0,16},{8,24},{16,0},{24,8},{1,17},{9,25},{17,1},{25,9},{2,18},{10... | collective-permute-start | bytes 786440 | tf_op jit(solution)/shard_map/ppermute | solution.py:544
  58.6 11.8 %collective-permute-start.3 = (bf16[256,512]{1,0:T(8,128)(2,1)S(1)}, bf16[256,512]{1,0:T(8,128)(2,1)}, u32[]{:S(2)}, u32[]{:S(2)}) collective-permute-start(bf16[256,512]{1,0:T(8,128)(2,1)S(1)} %copy-done), channel_id=1, source_target_pairs={{0,8},{8,0},{16,24},{24,16},{1,9},{9,1},{17,25},{25,17},{2,10},{10... | collective-permute-start | bytes 786440 | tf_op jit(solution)/shard_map/ppermute | solution.py:544
  70.3 0.7 copy-start.1
  96.3 3.5 %collective-permute-start.7 = (bf16[896,384]{1,0:T(8,128)(2,1)S(1)}, bf16[896,384]{1,0:T(8,128)(2,1)}, u32[]{:S(2)}, u32[]{:S(2)}) collective-permute-start(bf16[896,384]{1,0:T(8,128)(2,1)S(1)} %constant_dynamic-slice_fusion), channel_id=1, source_target_pairs={{0,8},{1,9},{2,10},{3,11},{4,12},{5,13},{6,14},{7,15},{8,0},{9,1},... | collective-permute-start | bytes 2064392 | tf_op jit(solution)/shard_map/ppermute | solution.py:489
  104.8 13.9 %collective-permute-start.8 = (bf16[1344,384]{1,0:T(8,128)(2,1)S(1)}, bf16[1344,384]{1,0:T(8,128)(2,1)}, u32[]{:S(2)}, u32[]{:S(2)}) collective-permute-start(bf16[1344,384]{1,0:T(8,128)(2,1)S(1)} %fusion), channel_id=1, source_target_pairs={{0,16},{1,17},{2,18},{3,19},{4,20},{5,21},{6,22},{7,23},{8,9},{9,8... | collective-permute-start | bytes 3096584 | tf_op jit(solution)/shard_map/ppermute | solution.py:489
  120.9 8.3 %collective-permute-start.9 = (bf16[672,384]{1,0:T(8,128)(2,1)S(1)}, bf16[672,384]{1,0:T(8,128)(2,1)S(1)}, u32[]{:S(2)}, u32[]{:S(2)}) collective-permute-start(bf16[672,384]{1,0:T(8,128)(2,1)S(1)} %add_convert_fusion.2), channel_id=1, source_target_pairs={{0,1},{1,0},{2,3},{3,2},{4,5},{5,4},{6,7},{7,6},{8,24},{9,25},{10,... | collective-permute-start | bytes 1548296 | tf_op jit(solution)/shard_map/ppermute | solution.py:489
  130.8 5.7 %collective-permute-start.10 = (bf16[336,384]{1,0:T(8,128)(2,1)S(1)}, bf16[336,384]{1,0:T(8,128)(2,1)S(1)}, u32[]{:S(2)}, u32[]{:S(2)}) collective-permute-start(bf16[336,384]{1,0:T(8,128)(2,1)S(1)} %add_convert_fusion.3), channel_id=1, source_target_pairs={{0,2},{1,3},{2,0},{3,1},{4,6},{5,7},{6,4},{7,5},{8,10},{9,11},{10,... | collective-permute-start | bytes 774152 | tf_op jit(solution)/shard_map/ppermute | solution.py:489
  137.6 5.5 %collective-permute-start.11 = (bf16[168,384]{1,0:T(8,128)(2,1)S(1)}, bf16[168,384]{1,0:T(8,128)(2,1)S(1)}, u32[]{:S(2)}, u32[]{:S(2)}) collective-permute-start(bf16[168,384]{1,0:T(8,128)(2,1)S(1)} %add_convert_fusion.5), channel_id=1, source_target_pairs={{0,4},{1,5},{2,6},{3,7},{4,0},{5,1},{6,2},{7,3},{8,12},{9,13},{10,... | collective-permute-start | bytes 387080 | tf_op jit(solution)/shard_map/ppermute | solution.py:489
  144.4 5.3 %collective-permute-start.12 = (bf16[168,384]{1,0:T(8,128)(2,1)S(1)}, bf16[168,384]{1,0:T(8,128)(2,1)S(1)}, u32[]{:S(2)}, u32[]{:S(2)}) collective-permute-start(bf16[168,384]{1,0:T(8,128)(2,1)S(1)} %add_convert_fusion.4), channel_id=1, source_target_pairs={{0,4},{1,5},{2,6},{3,7},{4,0},{5,1},{6,2},{7,3},{8,12},{9,13},{10,... | collective-permute-start | bytes 387080 | tf_op jit(solution)/shard_map/ppermute | solution.py:489
  149.8 6.5 %collective-permute-start.13 = (bf16[336,384]{1,0:T(8,128)(2,1)S(1)}, bf16[336,384]{1,0:T(8,128)(2,1)S(1)}, u32[]{:S(2)}, u32[]{:S(2)}) collective-permute-start(bf16[336,384]{1,0:T(8,128)(2,1)S(1)} %maximum_select_fusion.3), channel_id=1, source_target_pairs={{0,2},{1,3},{2,0},{3,1},{4,6},{5,7},{6,4},{7,5},{8,10},{9,11},{10,... | collective-permute-start | bytes 774152 | tf_op jit(solution)/shard_map/ppermute | solution.py:489
  156.4 8.0 %collective-permute-start.14 = (bf16[672,384]{1,0:T(8,128)(2,1)S(1)}, bf16[672,384]{1,0:T(8,128)(2,1)S(1)}, u32[]{:S(2)}, u32[]{:S(2)}) collective-permute-start(bf16[672,384]{1,0:T(8,128)(2,1)S(1)} %maximum_select_fusion.2), channel_id=1, source_target_pairs={{0,1},{1,0},{2,3},{3,2},{4,5},{5,4},{6,7},{7,6},{8,24},{9,25},{10,... | collective-permute-start | bytes 1548296 | tf_op jit(solution)/shard_map/ppermute | solution.py:489
  164.8 19.0 %collective-permute-start.15 = (bf16[1344,384]{1,0:T(8,128)(2,1)S(1)}, bf16[1344,384]{1,0:T(8,128)(2,1)S(1)}, u32[]{:S(2)}, u32[]{:S(2)}) collective-permute-start(bf16[1344,384]{1,0:T(8,128)(2,1)S(1)} %maximum_select_fusion.1), channel_id=1, source_target_pairs={{0,16},{1,17},{2,18},{3,19},{4,20},{5,21},{6,22},{7,23},{8,9},{9,8... | collective-permute-start | bytes 3096584 | tf_op jit(solution)/shard_map/ppermute | solution.py:489
  184.3 13.4 %collective-permute-start.16 = (bf16[2688,384]{1,0:T(8,128)(2,1)S(1)}, bf16[2688,384]{1,0:T(8,128)(2,1)S(1)}, u32[]{:S(2)}, u32[]{:S(2)}) collective-permute-start(bf16[2688,384]{1,0:T(8,128)(2,1)S(1)} %maximum_select_fusion), channel_id=1, source_target_pairs={{0,8},{1,9},{2,10},{3,11},{4,12},{5,13},{6,14},{7,15},{8,0},{9,1},... | collective-permute-start | bytes 6193160 | tf_op jit(solution)/shard_map/ppermute | solution.py:489

commit v2 on v1

--- a/solution.py
+++ b/solution.py
@@ -12,9 +12,10 @@
 F32 = jnp.float32
 LOG2E = math.log2(math.e)
 EPS = 1e-07
-VMEM_LIMIT = 56 * 1024 * 1024
+VMEM_LIMIT = 28 * 1024 * 1024
+FIRST_PAIRS = 2
 EARLY_ROWS = 3584
-LATE_ROWS = 1792
+LATE_ROWS = 2048
 
 
 def nn(left, right):
@@ -152,8 +153,12 @@
     return folded * scale
 
 
+def as_row(vector_ref):
+    return vector_ref[...].astype(F32).reshape(1, -1)
+
+
 def affine(values, weight_ref, bias_ref):
-    return nn(values, weight_ref[...]) + bias_ref[...].astype(F32)
+    return nn(values, weight_ref[...]) + as_row(bias_ref)
 
 
 def norm_forward(values):
@@ -174,25 +179,39 @@
 
 
 def forward_kernel(
-    block_ref, length_ref, own, core, far, diagonal,
-    query_weight, query_bias, key_weight, key_bias, value_weight, value_bias,
-    output_weight, output_bias, first_gain, first_bias, inner_weight, inner_bias,
-    outer_weight, outer_bias, second_gain, second_bias, relative, relative_back, cotangent,
-    layer_out, grad_first_out, chances_out, sent_out, query_out, key_out, value_out,
-    rel_query_out, rel_key_out, grads_out,
-    x_all, s_ref, mixture_ref, log_ref, active_ref, slope_ref,
+    block_ref, length_ref, relative, query_weight, key_weight, own, core, far, diagonal, value_weight,
+    output_weight, inner_weight, outer_weight, cotangent,
+    query_bias, key_bias, value_bias, output_bias, first_gain, first_bias, inner_bias, outer_bias,
+    second_gain, second_bias,
+    layer_store, first_store, chances_store, sent_store, query_store, key_store, value_store,
+    rel_query_store, rel_key_store, early_send_low, early_send_high, early_keep,
+    x_all, s_ref, mixture_ref, log_ref, active_ref, slope_ref, grads_out,
 ):
     block = block_ref[0]
     length = length_ref[0]
-    size, model_width = own.shape
+    size, model_width = layer_store.shape
+    query_bias, key_bias, value_bias = ready(query_bias, key_bias, value_bias)
     head_dim = model_width // HEADS
     factor = LOG2E / math.sqrt(3.0 * head_dim)
+    query_out, key_out, value_out = query_store.ref, key_store.ref, value_store.ref
+    rel_query_out, rel_key_out = rel_query_store.ref, rel_key_store.ref
+    chances_out, sent_out = chances_store.ref, sent_store.ref
+    relative, query_weight, key_weight = ready(relative, query_weight, key_weight)
+    rel_query_out[...] = affine(relative[...], query_weight, query_bias).astype(BF)
+    rel_query_store.push()
+    rel_key_out[...] = affine(
+        nn(reversal(relative.shape[0]), relative[...]).astype(BF), key_weight, key_bias
+    ).astype(BF)
+    rel_key_store.push()
+    own, core, far, diagonal = ready(own, core, far, diagonal)
     place_blocks(block, x_all, own, core, far, diagonal)
     query_out[...] = affine(x_all[...], query_weight, query_bias).astype(BF)
+    query_store.push()
     key_out[...] = affine(x_all[...], key_weight, key_bias).astype(BF)
+    key_store.push()
+    (value_weight,) = ready(value_weight)
     value_out[...] = affine(x_all[...], value_weight, value_bias).astype(BF)
-    rel_query_out[...] = affine(relative[...], query_weight, query_bias).astype(BF)
-    rel_key_out[...] = affine(relative_back[...], key_weight, key_bias).astype(BF)
+    value_store.push()
     step = lanes((1, 4 * size))
     position = ((block + 3 + step // size) % 4) * size + step % size
     mask_row = jnp.where(position < length, 0.0, -1e30)
@@ -231,31 +250,37 @@
 
     lax.fori_loop(0, HEADS // 2, pair_step, 0)
 
+    output_weight, inner_weight, outer_weight, cotangent = ready(output_weight, inner_weight, outer_weight, cotangent)
+    output_bias, first_gain, first_bias, inner_bias, outer_bias, second_gain, second_bias = ready(
+        output_bias, first_gain, first_bias, inner_bias, outer_bias, second_gain, second_bias
+    )
     inner_width = inner_weight.shape[1]
     chunks = inner_width // model_width
     mixture_low = mixture_ref[...].astype(BF)
     first_sum = own[...].astype(F32) + affine(mixture_low, output_weight, output_bias)
     first_hat, first_rate = norm_forward(first_sum)
-    normed = (first_hat * first_gain[...].astype(F32) + first_bias[...].astype(F32)).astype(BF)
+    normed = (first_hat * as_row(first_gain) + as_row(first_bias)).astype(BF)
     root_half = math.sqrt(0.5)
     density = 1.0 / math.sqrt(2.0 * math.pi)
 
-    second_sum = normed.astype(F32) + outer_bias[...].astype(F32)
+    inner_row = as_row(inner_bias)
+    second_sum = normed.astype(F32) + as_row(outer_bias)
     for chunk in range(chunks):
         span = slice(chunk * model_width, (chunk + 1) * model_width)
-        inner_pre = nn(normed, inner_weight[:, span]) + inner_bias[:, span].astype(F32)
+        inner_pre = nn(normed, inner_weight[:, span]) + inner_row[:, span]
         below = 0.5 + 0.5 * lax.erf(inner_pre * root_half)
         slope_ref[:, span] = below + inner_pre * density * jnp.exp(-0.5 * inner_pre * inner_pre)
         active_ref[:, span] = (inner_pre * below).astype(BF)
         second_sum = second_sum + nn(active_ref[:, span], outer_weight[span, :])
     second_hat, second_rate = norm_forward(second_sum)
-    gain = second_gain[...].astype(F32)
-    layer_out[...] = second_hat * gain + second_bias[...].astype(F32)
+    gain = as_row(second_gain)
+    layer_store.ref[...] = second_hat * gain + as_row(second_bias)
+    layer_store.push()
     cot = cotangent[...].astype(F32)
     grad_second = norm_backward(cot * gain, second_hat, second_rate)
     grad_outer = grad_second.astype(BF)
     outer_at, inner_at, output_at, small_at = 0, inner_width, 2 * inner_width, 2 * inner_width + model_width
-    grads_out[small_at:, :] = jnp.zeros((grads_out.shape[0] - small_at, model_width), BF)
+    grads_out[small_at + 16 :, :] = jnp.zeros((grads_out.shape[0] - small_at - 16, model_width), BF)
     small = [column_sum(grad_outer), column_sum(cot * second_hat), column_sum(cot)]
     grad_normed = grad_second
     for chunk in range(chunks):
@@ -270,13 +295,15 @@
         ).astype(BF)
         grad_normed = grad_normed + nt(grad_inner, inner_weight[:, span])
     grad_normed = grad_normed.astype(BF).astype(F32)
-    grad_first = norm_backward(grad_normed * first_gain[...].astype(F32), first_hat, first_rate)
-    grad_first_out[...] = grad_first
+    grad_first = norm_backward(grad_normed * as_row(first_gain), first_hat, first_rate)
+    first_store.ref[...] = grad_first
+    first_store.push()
     grad_branch = grad_first.astype(BF)
     grads_out[output_at : output_at + model_width, :] = tn(mixture_low, grad_branch).astype(BF)
     small += [column_sum(grad_normed * first_hat), column_sum(grad_normed), column_sum(grad_branch)]
     small += [jnp.zeros((16 - len(small), model_width), F32)]
     grads_out[small_at : small_at + 16, :] = jnp.concatenate(small, axis=0).astype(BF)
+    push_halves(block % 2, grads_out, (early_send_low, early_send_high), early_keep)
     grad_mixture = nt(grad_branch, output_weight[...]).astype(BF)
     sent_out[:, :model_width] = grad_mixture
     along = grad_mixture.astype(F32) * mixture_ref[...]
@@ -291,6 +318,7 @@
     group = stat_lane // 8
     parts = jnp.where((group == 0) | (group == 2), upper, jnp.where((group == 1) | (group == 3), middle, rest - middle))
     sent_out[:, model_width:] = jnp.where(group < 5, parts, 0.0).astype(BF)
+    sent_store.push()
 
 
 def position_backward(block, side, grad_scores, flip, other_pair, ext_pair, own_rows_back, wall_ref, near_ref, shift):
@@ -301,14 +329,16 @@
 
 
 def query_kernel(
-    block_ref, chances, sent, query_all, key_all, value_all, rel_key,
-    grad_query_out, grad_rel_key_out,
+    block_ref, rel_key, query_all, sent, value_all, key_all, chances_load,
+    query_store, rel_key_grad_store,
     ext_ref, wall_ref, near_ref, back_ref, sum_ref, rows_ref,
 ):
     block = block_ref[0]
-    size, model_width = grad_query_out.shape
+    size, model_width = query_store.shape
     scale = 1.0 / math.sqrt(3.0 * (model_width // HEADS))
     flip = reversal(size)
+    chances = chances_load.buffer
+    rel_key, query_all, sent, value_all, key_all = ready(rel_key, query_all, sent, value_all, key_all)
     extend_table(block, ext_ref, rel_key)
     back_ref[...] = nn(flip, query_all[size : 2 * size, :]).astype(BF)
     stats = sent[:, model_width:].astype(F32)
@@ -335,31 +365,28 @@
             else:
                 sum_ref[...] += table
         rows_ref[:, columns] = (row_grad * scale).astype(BF)
-        grad_rel_key_out[columns, :] = table_grad(block, sum_ref[...], scale)
+        rel_key_grad_store.ref[columns, :] = table_grad(block, sum_ref[...], scale)
         return carry
 
     lax.fori_loop(0, HEADS // 2, pair_step, 0)
-    grad_query_out[...] = nn(flip, rows_ref[...]).astype(BF)
-
-
-def key_kernel(
-    block_ref, length_ref, own, sent_own, sent_core, sent_far, sent_diagonal, query_all, key_all, value_all,
-    rel_query, rel_key, grad_query, grad_rel_key, grad_first,
-    query_weight, key_weight, value_weight, relative,
-    grad_tokens_out, grads_out,
-    sent_ref, s_ref, grad_ref, ext_ref, wall_ref, near_ref, back_ref, sum_ref, key_rows_ref, value_rows_ref,
-    rel_grad_ref, stat_ref,
+    query_store.ref[...] = nn(flip, rows_ref[...]).astype(BF)
+
+
+def key_pairs(
+    first, last, block_ref, length_ref, rel_query, key_all, rel_key, query_all, value_all,
+    sent_own, sent_core, sent_far, sent_diagonal, key_rows_ref, value_rows_ref, rel_grad_ref,
+    sent_ref, s_ref, grad_ref, ext_ref, wall_ref, near_ref, back_ref, sum_ref, stat_ref,
 ):
     block = block_ref[0]
     length = length_ref[0]
-    size, model_width = own.shape
-    rel = rel_query.shape[0]
+    size, model_width = key_rows_ref.shape
     scale = 1.0 / math.sqrt(3.0 * (model_width // HEADS))
     factor = LOG2E * scale
     flip = reversal(size)
-    place_blocks(block, sent_ref, sent_own, sent_core, sent_far, sent_diagonal)
+    rel_query, key_all, rel_key, query_all, value_all = ready(rel_query, key_all, rel_key, query_all, value_all)
     extend_table(block, ext_ref, rel_query)
     back_ref[...] = nn(flip, key_all[size : 2 * size, :]).astype(BF)
+    place_blocks(block, sent_ref, *ready(sent_own, sent_core, sent_far, sent_diagonal))
     stats = sent_ref[:, model_width:].astype(F32).T
     stat_ref[0:8, :] = stats[0:8, :] + stats[8:16, :]
     stat_ref[8:16, :] = stats[16:24, :] + (stats[24:32, :] + stats[32:40, :])
@@ -372,18 +399,18 @@
         value_grad = jnp.zeros((size, 128), F32)
         for side in range(2):
             head = 2 * pair + side
-            key_own = of_head(key_all[size : 2 * size, columns], side)
+            key_head = of_head(key_all[size : 2 * size, columns], side)
             position_terms(
                 block,
                 s_ref,
-                key_own,
+                key_head,
                 rel_query[:, columns],
                 lambda slot: query_all[slot * size : (slot + 1) * size, columns],
                 of_head(rel_key[:, columns], side),
                 0,
                 1,
             )
-            content = nt(key_own, query_all[:, columns])
+            content = nt(key_head, query_all[:, columns])
             shift = mask_column - stat_ref[pl.ds(8 + head, 1), :]
             s_ref[...] = jnp.exp2((s_ref[...] + content) * factor + shift)
             value_grad = value_grad + nn(s_ref[...].astype(BF), of_head(sent_ref[:, columns], side))
@@ -403,8 +430,35 @@
         rel_grad_ref[columns, :] = table_grad(block, sum_ref[...], scale)
         return carry
 
-    lax.fori_loop(0, HEADS // 2, pair_step, 0)
-    grad_key = nn(flip, key_rows_ref[...]).astype(BF)
+    lax.fori_loop(first, last, pair_step, 0)
+
+
+def first_key_kernel(*refs):
+    ins, outs, scratch = refs[:11], refs[11:14], refs[14:]
+    key_pairs(0, FIRST_PAIRS, *ins, *(out.ref for out in outs), *scratch)
+
+
+def last_key_kernel(*refs):
+    ins, before, outs, scratch = refs[:11], refs[11:14], refs[14:17], refs[17:]
+    done = FIRST_PAIRS * 128
+    for old, out in zip(ready(*before), outs):
+        if out.shape[0] == outs[0].shape[0]:
+            out.ref[:, :done] = old[:, :done]
+        else:
+            out.ref[:done, :] = old[:done, :]
+    key_pairs(FIRST_PAIRS, HEADS // 2, *ins, *(out.ref for out in outs), *scratch)
+
+
+def final_kernel(
+    block_ref, own, relative, key_rows, value_rows, rel_grad, grad_query, grad_rel_key, query_weight, key_weight,
+    value_weight, grad_first, tokens_store, late_send_low, late_send_high, late_keep, grads_out,
+):
+    size, model_width = tokens_store.shape
+    own, relative, key_rows_ref, value_rows_ref, rel_grad_ref, grad_query, grad_rel_key = ready(
+        own, relative, key_rows, value_rows, rel_grad, grad_query, grad_rel_key
+    )
+    rel = relative.shape[0]
+    grad_key = nn(reversal(size), key_rows_ref[...]).astype(BF)
     grad_value = value_rows_ref[...]
     rel_query_grad = rel_grad_ref[...]
     rel_key_grad = grad_rel_key[...]
@@ -416,11 +470,12 @@
     grads_out[model_width : 2 * model_width, :] = (tn(tokens, grad_key) + tt(table, key_low)).astype(BF)
     grads_out[2 * model_width : 3 * model_width, :] = tn(tokens, grad_value).astype(BF)
     table_at = 3 * model_width
+    query_weight, key_weight, value_weight, grad_first = ready(query_weight, key_weight, value_weight, grad_first)
     grads_out[table_at : table_at + rel, :] = (
         tt(query_low, query_weight[...]) + tt(key_low, key_weight[...])
     ).astype(BF)
     small_at = table_at + rel
-    grads_out[small_at:, :] = jnp.zeros((grads_out.shape[0] - small_at, model_width), BF)
+    grads_out[small_at + 16 :, :] = jnp.zeros((grads_out.shape[0] - small_at - 16, model_width), BF)
     ones = jnp.ones((8, rel), BF)
 
     def lane_sums(values):
@@ -435,7 +490,8 @@
         jnp.zeros((13, model_width), F32),
     ]
     grads_out[small_at : small_at + 16, :] = jnp.concatenate(small, axis=0).astype(BF)
-    grad_tokens_out[...] = (
+    push_halves(block_ref[0] % 2, grads_out, (late_send_low, late_send_high), late_keep)
+    tokens_store.ref[...] = (
         nt(grad_query[...], query_weight[...])
         + nt(grad_key, key_weight[...])
         + nt(grad_value, value_weight[...])
@@ -443,89 +499,269 @@
     )
 
 
-def call(kernel, outs, scratch, *operands, scalars):
-    in_specs = [pl.BlockSpec(memory_space=pltpu.SMEM)] * scalars
-    in_specs += [pl.BlockSpec(memory_space=pltpu.VMEM)] * (len(operands) - scalars)
+class Load:
+    def __init__(self, source, buffer, sem):
+        self.copy, self.buffer, self.waiting = pltpu.make_async_copy(source, buffer, sem), buffer, True
+        self.copy.start()
+
+    def ready(self):
+        if self.waiting:
+            self.copy.wait()
+        self.waiting = False
+        return self.buffer
+
+
+def ready(*loads):
+    return [load.ready() for load in loads]
+
+
+class Store:
+    def __init__(self, target, buffer, sem):
+        self.copy, self.ref, self.shape, self.waiting = pltpu.make_async_copy(buffer, target, sem), buffer, buffer.shape, False
+
+    def push(self):
+        self.copy.start()
+        self.waiting = True
+
+    def finish(self):
+        if not self.waiting:
+            self.push()
+        self.copy.wait()
+
+
+class Here:
+    def __init__(self, ref):
+        self.ref = self.buffer = ref
+        self.shape = ref.shape
+
+    def ready(self):
+        return self.ref
+
+    def push(self):
+        pass
+
+    def finish(self):
+        pass
+
+
+class Raw:
+    def __init__(self, target, sem):
+        self.target, self.sem = target, sem
+        self.shape = target.shape
+
+    def push_from(self, source):
+        self.copy = pltpu.make_async_copy(source, self.target, self.sem)
+        self.copy.start()
+
+    def finish(self):
+        self.copy.wait()
+
+
+def push_halves(core, rows_ref, sends, keep):
+    half = keep.shape[0]
+    for k, send in enumerate(sends):
+        at = (1 - core) * half + k * send.shape[0]
+        send.push_from(rows_ref.at[pl.ds(pl.multiple_of(at, 16), send.shape[0])])
+    keep.push_from(rows_ref.at[pl.ds(pl.multiple_of(core * half, 16), half)])
+
+
+class Kept:
+    def __init__(self, *what):
+        self.what = what
+
+
+def call(kernel, outs, scratch, *operands, scalars, micros):
+    kept_in = [isinstance(operand, Kept) for operand in operands]
+    kept_out = [isinstance(out, Kept) for out in outs]
+    operands = [
+        operand if k < scalars
+        else pltpu.with_memory_space_constraint(operand.what[0], pltpu.VMEM) if kept
+        else pltpu.with_memory_space_constraint(operand, pltpu.HBM)
+        for k, (operand, kept) in enumerate(zip(operands, kept_in))
+    ]
+    outs = [out.what if kept else out for out, kept in zip(outs, kept_out)]
+    raw = [len(out) > 2 for out in outs]
+    loads = [k for k in range(scalars, len(operands)) if not kept_in[k]]
+    stores = [k for k in range(len(outs)) if not kept_out[k]]
+    buffered = [k for k in stores if not raw[k]]
+
+    def body(*refs):
+        n, m = len(operands), len(outs)
+        ins, results, rest = list(refs[:n]), list(refs[n : n + m]), list(refs[n + m :])
+        in_sems, out_sems = rest.pop(), rest.pop()
+        buffers = [rest.pop() for _ in range(len(loads) + len(buffered))][::-1]
+        for k in range(scalars, n):
+            if kept_in[k]:
+                ins[k] = Here(ins[k])
+        for place, k in enumerate(loads):
+            ins[k] = Load(ins[k], buffers[place], in_sems.at[place])
+        buffers = buffers[len(loads) :]
+        for k in range(m):
+            if kept_out[k]:
+                results[k] = Here(results[k])
+        for place, k in enumerate(stores):
+            if raw[k]:
+                results[k] = Raw(results[k], out_sems.at[place])
+            else:
+                results[k] = Store(results[k], buffers.pop(0), out_sems.at[place])
+        kernel(*ins, *results, *rest)
+        for k in stores:
+            results[k].finish()
+
+    spaces = [
+        pltpu.SMEM if k < scalars else pltpu.VMEM if kept_in[k] else pltpu.HBM for k in range(len(operands))
+    ]
+    buffers = [(operands[k].shape, operands[k].dtype) for k in loads] + [outs[k][:2] for k in buffered]
     return pl.pallas_call(
-        kernel,
-        out_shape=[jax.ShapeDtypeStruct(shape, kind) for shape, kind in outs],
-        in_specs=in_specs,
-        out_specs=[pl.BlockSpec(memory_space=pltpu.VMEM)] * len(outs),
-        scratch_shapes=[pltpu.VMEM(shape, kind) for shape, kind in scratch],
+        body,
+        out_shape=[
+            pltpu.VMEM(out[0], out[1]) if kept else pltpu.HBM(out[0], out[1])
+            for out, kept in zip(outs, kept_out)
+        ],
+        in_specs=[pl.BlockSpec(memory_space=space) for space in spaces],
+        out_specs=[pl.BlockSpec(memory_space=pltpu.VMEM if kept else pltpu.HBM) for kept in kept_out],
+        scratch_shapes=[pltpu.VMEM(shape, kind) for shape, kind in list(scratch) + buffers]
+        + [pltpu.SemaphoreType.DMA((max(len(stores), 1),)), pltpu.SemaphoreType.DMA((max(len(loads), 1),))],
         compiler_params=pltpu.CompilerParams(vmem_limit_bytes=VMEM_LIMIT),
+        cost_estimate=pl.CostEstimate(flops=micros * 10**9, bytes_accessed=micros * 10**6, transcendentals=0),
     )(*operands)
 
 
-def hop_table(blk_count, dp_count, bit_of):
-    pairs = []
-    for blk in range(blk_count):
-        for dp in range(dp_count):
-            axis, bit = bit_of(blk)
-            there = (blk ^ bit, dp) if axis == 0 else (blk, dp ^ bit)
-            pairs.append((blk * dp_count + dp, there[0] * dp_count + there[1]))
-    return pairs
-
-
-def all_sum(early, late, blk_count, dp_count):
-    both = ("blk", "dp")
-    blk, dp = lax.axis_index("blk"), lax.axis_index("dp")
-    steps = [lambda b: (0, 1)]
-    first, second = (0, 2), (1, 1)
-    steps.append(lambda b: first if b % 2 == 0 else second)
-    steps.append(lambda b: second if b % 2 == 0 else first)
-    bit = 2
+class Group:
+    def __init__(self, blk_count, dp_count, bits):
+        self.blk_count, self.dp_count, self.bits = blk_count, dp_count, bits
+        self.size = 2 ** len(bits)
+        place = {"blk": lax.axis_index("blk"), "dp": lax.axis_index("dp")}
+        self.digits = [(place[axis] >> (bit.bit_length() - 1)) & 1 for axis, bit in bits]
+        self.me = sum(digit << k for k, digit in enumerate(self.digits))
+
+    def pairs(self, mask):
+        change = {"blk": 0, "dp": 0}
+        for k, (axis, bit) in enumerate(self.bits):
+            if mask >> k & 1:
+                change[axis] |= bit
+        return [
+            (blk * self.dp_count + dp, (blk ^ change["blk"]) * self.dp_count + (dp ^ change["dp"]))
+            for blk in range(self.blk_count)
+            for dp in range(self.dp_count)
+        ]
+
+    def send(self, values, mask):
+        return lax.ppermute(values, ("blk", "dp"), self.pairs(mask))
+
+    def scatter(self, terms):
+        def part(index):
+            return [
+                (array, first + index * (blocks // self.size), blocks // self.size) for array, first, blocks in terms
+            ]
+
+        outs = [total(part(self.me ^ mask)) for mask in range(1, self.size)]
+        arrived = [self.send(out, mask + 1) for mask, out in enumerate(outs)]
+        return outs, part(self.me) + [whole(array) for array in arrived]
+
+    def pieces(self, held):
+        return [held] + [self.send(held, mask) for mask in range(1, self.size)]
+
+    def gather(self, held):
+        parts = self.pieces(held)
+        for k, digit in enumerate(self.digits):
+            parts = [
+                jnp.where(digit == 0, parts[q], parts[q ^ (1 << k)]) for q in range(self.size)
+            ]
+        return jnp.concatenate(parts, axis=0)
+
+
+def groups_of(blk_count, dp_count):
+    bits, bit = [], 2
     while bit < dp_count:
-        steps.append(lambda b, bit=bit: (1, bit))
+        bits.append(("dp", bit))
         bit *= 2
-
-    def my_bit(step):
-        axis0, bit0 = step(0)
-        axis1, bit1 = step(1)
-        even = (blk if axis0 == 0 else dp) // bit0 % 2
-        odd = (blk if axis1 == 0 else dp) // bit1 % 2
-        return jnp.where(blk % 2 == 0, even, odd)
-
-    def exchange(values, step):
-        return lax.ppermute(values, both, hop_table(blk_count, dp_count, step))
-
-    bit = my_bit(steps[0])
-
-    def half(values, which):
-        rows = values.shape[0] // 2
-        return lax.dynamic_slice_in_dim(values, which * rows, rows, 0)
-
-    early_in = exchange(half(early, 1 - bit), steps[0])
-    late_in = exchange(half(late, 1 - bit), steps[0])
-    mine = jnp.concatenate(
-        [
-            half(early, bit).astype(F32) + early_in.astype(F32),
-            half(late, bit).astype(F32) + late_in.astype(F32),
-        ],
-        axis=0,
-    )
-    terms = [mine.astype(BF)]
-    for step in steps[1:]:
-        bit = my_bit(step)
-        send = sum(half(t, 1 - bit).astype(F32) for t in terms).astype(BF)
-        arrived = exchange(send, step)
-        terms = [half(t, bit) for t in terms] + [arrived]
-    held = sum(t.astype(F32) for t in terms).astype(BF)
-    for step in reversed(steps[1:]):
-        bit = my_bit(step)
-        arrived = exchange(held, step)
-        rows = held.shape[0]
-        held = jnp.where(
-            bit == 0, jnp.concatenate([held, arrived], axis=0), jnp.concatenate([arrived, held], axis=0)
-        )
-    bit = my_bit(steps[0])
-    arrived = exchange(held, steps[0])
-    low = jnp.where(bit == 0, held, arrived)
-    high = jnp.where(bit == 0, arrived, held)
-    cut = early.shape[0] // 2
-    return (
-        jnp.concatenate([low[:cut], high[:cut]], axis=0).astype(F32),
-        jnp.concatenate([low[cut:], high[cut:]], axis=0).astype(F32),
-    )
+    groups = [[("blk", 1)], [("blk", 2), ("dp", 1)]]
+    groups += [bits[k : k + 2] for k in range(0, len(bits), 2)]
+    return [Group(blk_count, dp_count, group) for group in groups]
+
+
+def whole(array):
+    return array, 0, array.shape[0]
+
+
+def total(terms):
+    spans = []
+    for array, first, blocks in terms:
+        if isinstance(array, tuple):
+            low, high = array
+            size = low.shape[0]
+            low = lax.dynamic_slice_in_dim(low, jnp.minimum(first, size - blocks), blocks, 0)
+            high = lax.dynamic_slice_in_dim(high, jnp.maximum(first - size, 0), blocks, 0)
+            spans.append(jnp.where(first < size, low, high))
+        else:
+            spans.append(lax.dynamic_slice_in_dim(array, first, blocks, 0))
+    return sum(span.astype(F32) for span in spans).astype(BF)
+
+
+def in_order(first, then):
+    return lax.optimization_barrier((first, then))[1]
+
+
+def halves_to_scratch(core_ref, held, arrived, both_ref):
+    held, arrived = ready(held, arrived)
+    rows = held.shape[0]
+    mine = pl.multiple_of(core_ref[0] * rows, 16)
+    theirs = pl.multiple_of((1 - core_ref[0]) * rows, 16)
+    both_ref[pl.ds(mine, rows), :] = held[...]
+    both_ref[pl.ds(theirs, rows), :] = arrived[...]
+
+
+def early_kernel(
+    core_ref, held, arrived,
+    outer_weight, inner_weight, output_weight, outer_bias, second_gain, second_bias, inner_bias, first_gain, first_bias,
+    output_bias,
+    both_ref,
+):
+    halves_to_scratch(core_ref, held, arrived, both_ref)
+    inner_width, width = outer_weight.shape
+    chunks = inner_width // width
+    outer_weight.ref[...] = both_ref[:inner_width, :].astype(F32)
+    outer_weight.push()
+    for chunk in range(chunks):
+        at = inner_width + chunk * width
+        inner_weight.ref[:, chunk * width : (chunk + 1) * width] = both_ref[at : at + width, :].astype(F32)
+    at = 2 * inner_width
+    output_weight.ref[...] = both_ref[at : at + width, :].astype(F32)
+    output_weight.push()
+    small = both_ref[at + width : at + width + 16, :].astype(F32)
+
+    def vector(out, row):
+        out.ref[...] = small[row, :]
+        out.push()
+
+    vector(outer_bias, 0)
+    vector(second_gain, 1)
+    vector(second_bias, 2)
+    inner_bias.ref[...] = jnp.concatenate([small[3 + k : 4 + k, :] for k in range(chunks)], axis=1)[0, :]
+    inner_bias.push()
+    vector(first_gain, 3 + chunks)
+    vector(first_bias, 4 + chunks)
+    vector(output_bias, 5 + chunks)
+
+
+def late_kernel(
+    core_ref, held, arrived,
+    query_weight, query_bias, key_weight, key_bias, value_weight, value_bias, relative,
+    both_ref,
+):
+    halves_to_scratch(core_ref, held, arrived, both_ref)
+    width = query_weight.shape[0]
+    rel = relative.shape[0]
+    for k, out in enumerate((query_weight, key_weight, value_weight)):
+        out.ref[...] = both_ref[k * width : (k + 1) * width, :].astype(F32)
+        out.push()
+    at = 3 * width
+    relative.ref[...] = both_ref[at : at + rel, :].astype(F32)
+    small = both_ref[at + rel : at + rel + 16, :].astype(F32)
+    query_bias.ref[...] = small[0, :]
+    key_bias.ref[...] = small[1, :]
+    value_bias.ref[...] = small[2, :]
 
 
 def on_device(
@@ -539,33 +775,45 @@
     inner_width = inner_weight.shape[1]
     own = tokens[0]
     block = lax.axis_index("blk").astype(jnp.int32).reshape(1)
+    groups = groups_of(blk_count, dp_count)
+    chips = groups[1:]
+    shards = blk_count * dp_count
 
     def along(values, bit):
         return lax.ppermute(values, "blk", [(i, i ^ bit) for i in range(blk_count)])
 
-    def row(vector):
-        return vector.reshape(1, -1)
+    def blocks(rows, share):
+        return rows.reshape(shards // share, -1, width)
+
+    def first_terms(keep, low, high):
+        arrived = tuple(groups[0].send(blocks(piece, 4), 1) for piece in (low, high))
+        return [whole(blocks(keep, 2)), (arrived, 0, shards // 2)]
+
+    def flat(values):
+        return values.reshape(-1, width)
 
     far = along(own, 2)
     core = along(own, 1)
     diagonal = along(far, 1)
-    relative_back = jnp.flip(relative_table, 0)
     full = blk_count * size
     (
-        layer_out, grad_first, chances, sent, query_all, key_all, value_all, rel_query, rel_key, early,
+        layer_out, grad_first, chances, sent, query_all, key_all, value_all, rel_query, rel_key,
+        early_send_low, early_send_high, early_keep,
     ) = call(
         forward_kernel,
         [
             ((size, width), F32),
-            ((size, width), F32),
-            ((HEADS, size, full), BF),
-            ((size, width + 128), BF),
-            ((full, width), BF),
-            ((full, width), BF),
-            ((full, width), BF),
-            ((rel, width), BF),
-            ((rel, width), BF),
-            ((EARLY_ROWS, width), BF),
+            Kept((size, width), F32),
+            Kept((HEADS, size, full), BF),
+            Kept((size, width + 128), BF),
+            Kept((full, width), BF),
+            Kept((full, width), BF),
+            Kept((full, width), BF),
+            Kept((rel, width), BF),
+            Kept((rel, width), BF),
+            ((EARLY_ROWS // 4, width), BF, "raw"),
+            ((EARLY_ROWS // 4, width), BF, "raw"),
+            ((EARLY_ROWS // 2, width), BF, "raw"),
         ],
         [
             ((full, width), BF),
@@ -574,73 +822,94 @@
             ((size, 128), F32),
             ((size, inner_width), BF),
             ((size, inner_width), F32),
+            ((EARLY_ROWS, width), BF),
         ],
-        block, lengths, own, core, far, diagonal,
-        query_weight, row(query_bias), key_weight, row(key_bias), value_weight, row(value_bias),
-        output_weight, row(output_bias), row(first_gain), row(first_bias), inner_weight, row(inner_bias),
-        outer_weight, row(outer_bias), row(second_gain), row(second_bias), relative_table, relative_back,
-        cotangent[0],
-        scalars=2,
-    )
+        block, lengths, relative_table, query_weight, key_weight, own, Kept(core), Kept(far), Kept(diagonal), value_weight,
+        output_weight, inner_weight, outer_weight, cotangent[0],
+        query_bias, key_bias, value_bias, output_bias, first_gain, first_bias, inner_bias, outer_bias,
+        second_gain, second_bias,
+        scalars=2, micros=27,
+    )
+    early_terms = first_terms(early_keep, early_send_low, early_send_high)
     sent_far = along(sent, 2)
     sent_core = along(sent, 1)
     sent_diagonal = along(sent, 3)
-    shared_scratch = [
+    position_scratch = [
         ((3 * rel, width), BF),
         ((size, 3 * rel), BF),
         ((size, full), BF),
         ((size, width), BF),
         ((128, 3 * rel), F32),
-        ((size, width), BF),
     ]
     grad_query, grad_rel_key = call(
         query_kernel,
-        [((size, width), BF), ((width, rel), F32)],
-        shared_scratch,
-        block, chances, sent, query_all, key_all, value_all, rel_key,
-        scalars=1,
-    )
-    grad_tokens, late = call(
-        key_kernel,
-        [((size, width), F32), ((LATE_ROWS, width), BF)],
-        [((full, width + 128), BF), ((size, full), F32), ((size, full), BF)]
-        + shared_scratch
-        + [((size, width), BF), ((width, rel), F32), ((16, full), F32)],
-        block, lengths, own, sent, sent_core, sent_far, sent_diagonal, query_all, key_all, value_all,
-        rel_query, rel_key, grad_query, grad_rel_key, grad_first,
-        query_weight, key_weight, value_weight, relative_table,
-        scalars=2,
-    )
-    early, late = all_sum(early, late, blk_count, dp_count)
-    inner_at, output_at = inner_width, 2 * inner_width
-    small_at = output_at + width
-    small = early[small_at : small_at + 16]
-    late_at = 3 * width + rel
-    late_small = late[late_at : late_at + 16]
-    g_inner_weight = jnp.concatenate(
-        [early[inner_at + k * width : inner_at + (k + 1) * width] for k in range(inner_width // width)], axis=1
-    )
-    chunks = inner_width // width
+        [Kept((size, width), BF), Kept((width, rel), F32)],
+        position_scratch + [((size, width), BF)],
+        block, *map(Kept, (rel_key, query_all, sent, value_all, key_all, chances)),
+        scalars=1, micros=8,
+    )
+    key_scratch = (
+        [((full, width + 128), BF), ((size, full), F32), ((size, full), BF)] + position_scratch + [((16, full), F32)]
+    )
+    key_arrays = tuple(
+        map(Kept, (rel_query, key_all, rel_key, query_all, value_all, sent, sent_core, sent_far, sent_diagonal))
+    )
+    key_outs = [Kept((size, width), BF), Kept((size, width), BF), Kept((width, rel), F32)]
+    sending, early_terms = chips[0].scatter(early_terms)
+    key_rows, value_rows, rel_grad = call(
+        first_key_kernel, key_outs, key_scratch, in_order(sending, block), lengths, *key_arrays,
+        scalars=2, micros=13,
+    )
+    for group in chips[1:]:
+        sending, early_terms = group.scatter(early_terms)
+    key_parts = call(
+        last_key_kernel, key_outs, key_scratch, in_order(sending, block), lengths, *key_arrays,
+        *map(Kept, (key_rows, value_rows, rel_grad)), scalars=2, micros=8,
+    )
+    early_held = total(early_terms)
+    grad_tokens, late_send_low, late_send_high, late_keep = call(
+        final_kernel,
+        [((size, width), F32)] + [((LATE_ROWS // 4, width), BF, "raw")] * 2 + [((LATE_ROWS // 2, width), BF, "raw")],
+        [((LATE_ROWS, width), BF)],
+        in_order(early_held, block), own, relative_table, *map(Kept, (*key_parts, grad_query, grad_rel_key)), query_weight,
+        key_weight, value_weight, Kept(grad_first),
+        scalars=1, micros=4,
+    )
+    for group in reversed(chips[1:]):
+        early_held = group.gather(early_held)
+    late_terms = first_terms(late_keep, late_send_low, late_send_high)
+    for group in chips:
+        sending, late_terms = group.scatter(late_terms)
+    early_held = chips[0].gather(in_order(sending, early_held))
+    late_held = total(late_terms)
+    for group in reversed(chips):
+        late_held = group.gather(late_held)
+    my_core = groups[0].me.astype(jnp.int32).reshape(1)
+    square, vector = ((width, width), F32), ((width,), F32)
+    (
+        g_outer_weight, g_inner_weight, g_output_weight, g_outer_bias, g_second_gain, g_second_bias, g_inner_bias,
+        g_first_gain, g_first_bias, g_output_bias,
+    ) = call(
+        early_kernel,
+        [((inner_width, width), F32), ((width, inner_width), F32), square, vector, vector, vector,
+         ((inner_width,), F32), vector, vector, vector],
+        [((EARLY_ROWS, width), BF)],
+        my_core, *(Kept(flat(piece)) for piece in groups[0].pieces(early_held)),
+        scalars=1, micros=4,
+    )
+    (
+        g_query_weight, g_query_bias, g_key_weight, g_key_bias, g_value_weight, g_value_bias, g_relative,
+    ) = call(
+        late_kernel,
+        [square, vector, square, vector, square, vector, ((rel, width), F32)],
+        [((LATE_ROWS, width), BF)],
+        my_core, *(Kept(flat(piece)) for piece in groups[0].pieces(late_held)),
+        scalars=1, micros=2,
+    )
     return (
-        layer_out[None],
-        grad_tokens[None],
-        late[0:width],
-        late_small[0],
-        late[width : 2 * width],
-        late_small[1],
-        late[2 * width : 3 * width],
-        late_small[2],
-        early[output_at : output_at + width],
-        small[5 + chunks],
-        small[3 + chunks],
-        small[4 + chunks],
-        g_inner_weight,
-        small[3 : 3 + chunks].reshape(-1),
-        early[0:inner_width],
-        small[0],
-        small[1],
-        small[2],
-        late[3 * width : 3 * width + rel],
+        layer_out[None], grad_tokens[None], g_query_weight, g_query_bias, g_key_weight, g_key_bias,
+        g_value_weight, g_value_bias, g_output_weight, g_output_bias, g_first_gain, g_first_bias,
+        g_inner_weight, g_inner_bias, g_outer_weight, g_outer_bias, g_second_gain, g_second_bias, g_relative,
     )
 
 

time: 207 us -> 151 us (0.73)
  waiting for transfers between devices: 69.2 us -> 29.5 us
  local copies, waits for them, and re-layouts: 27.9 us -> 0.01 us
  starting transfers between devices: 31 us -> 47.5 us
  other arithmetic: 15.3 us -> 5.63 us
  Pallas kernels: 61.1 us -> 63.8 us
    ppermute x11 -> x30, waiting for transfers between devices: 65.4 us -> 25.4 us  [send(): return lax.ppermute(values, ('blk', 'dp'), self.pairs(mask))]
    ppermute x11 -> x30, starting transfers between devices: 25 us -> 40.8 us  [send(): return lax.ppermute(values, ('blk', 'dp'), self.pairs(mask))]
    reshape x11 -> x0, local copies, waits for them, and re-layouts: 13.1 us -> none  [the longest x10 12.5 us: row(): return vector.reshape(1, -1)]
    rev x1 -> x0, local copies, waits for them, and re-layouts: 6.34 us -> none  [on_device(): relative_back = jnp.flip(relative_table, 0)]
    slice x7 -> x0, local copies, waits for them, and re-layouts: 4.43 us -> none  [the longest x1 1.56 us: on_device(): early[0:inner_width]]
    another operation x2 -> x0, other arithmetic: 3.17 us -> none
    concatenate x2 -> x4, other arithmetic: 3.47 us -> 0.44 us  [gather(): return jnp.concatenate(parts, axis=0)]
    dynamic_slice x2 -> x0, local copies, waits for them, and re-layouts: 2.69 us -> none  [half(): return lax.dynamic_slice_in_dim(values, which * rows, rows, 0)]
  transfers between devices with their start and end apart: 17 -> 36, of which waited for: 12 -> 14; matrix products, arithmetic and copies ran while one was open for 10% -> 2% of each run, Pallas kernels for 17% -> 21%
where the time goes in v2:
time: 151 us; the launch traced here: 148 us
  Pallas kernels  63.8 us (42%)
  starting transfers between devices  47.5 us (31%)
  waiting for transfers between devices  29.5 us (20%)
  other arithmetic  5.63 us (4%)
  between operations  1.79 us (1%)
    pallas_call x7, Pallas kernels, call(): pl.pallas_call(body, out_shape=[pltpu.VMEM(out[0], out[1]) if kept else p...  63.8 us
    ppermute x30, starting transfers between devices, send(): return lax.ppermute(values, ('blk', 'dp'), self.pairs(mask))  40.8 us
    ppermute x30, waiting for transfers between devices, send(): return lax.ppermute(values, ('blk', 'dp'), self.pairs(mask))  25.4 us
    ppermute x6, starting transfers between devices, along(): return lax.ppermute(values, 'blk', [(i, i ^ bit) for i in range(blk_count)])  6.68 us
    convert_element_type x8, other arithmetic, total(): return sum((span.astype(F32) for span in spans)).astype(BF)  4.75 us
    ppermute x6, waiting for transfers between devices, along(): return lax.ppermute(values, 'blk', [(i, i ^ bit) for i in range(blk_count)])  4.15 us
  transfers between devices with their start and end apart: 36, of which 14 were waited for; matrix products, arithmetic and copies ran while one was open for 2% of the time, Pallas kernels for 21%

profile of v2, /device:TPU:9, one launch (start us, length us, event | category | flops | bytes accessed | tf_op | source)
XLA Modules:
  0.0 148.2 jit_solution(9406563391547756638)
XLA Ops:
  2.9 3.8 %collective-permute-done.1.refs_7_ = bf16[256,384]{1,0:T(8,128)(2,1)S(1)} collective-permute-done((bf16[256,384]{1,0:T(8,128)(2,1)}, bf16[256,384]{1,0:T(8,128)(2,1)S(1)}, u32[]{:S(2)}, u32[]{:S(2)}) %collective-permute-start.1) | collective-permute-done | bytes 196640 | tf_op jit(solution)/shard_map/ppermute | solution.py:783
  9.3 24.9 %shard_map.339 = (f32[256,384]{1,0:T(8,128)}, f32[256,384]{1,0:T(8,128)S(1)}, bf16[6,256,1024]{2,1,0:T(8,128)(2,1)S(1)}, bf16[256,512]{1,0:T(8,128)(2,1)S(1)}, b...) custom-call(s32[1]{0:T(128)} %bitcast.refs_0_, ...), custom_call_target="tpu_custom_call" | custom-call | flops 27000000512 | bytes 27000000 | tf_op jit(solution)/shard_map/pallas_call | solution.py:615
  37.7 7.8 %shard_map.342 = (bf16[256,384]{1,0:T(8,128)(2,1)S(1)}, f32[384,512]{1,0:T(8,128)S(1)}) custom-call(s32[1]{0:T(128)} %bitcast.refs_0_, bf16[512,384]{1,0:T(8,128)(2,1)S(1)} %get-tuple-element.72.refs_4_.refs_1_, bf16[1024,384]{1,0:T(8,128)(2,1)S(1)} %get-tuple-element.73.refs_5_.refs_2_, bf16[256,512]{1,0:T(8,128)(2,1)S(1)} %get-tuple-element.75.refs_7_.refs_3_, ...), custom_call_target="tpu_custom_call" | custom-call | flops 8000000000 | bytes 8000000 | tf_op jit(solution)/shard_map/pallas_call | solution.py:615
  45.9 1.9 %collective-permute-start.5 = (bf16[4,112,384]{2,1,0:T(8,128)(2,1)S(1)}, bf16[4,112,384]{2,1,0:T(8,128)(2,1)S(1)}, u32[]{:S(2)}, u32[]{:S(2)}) collective-permute-start(bf16[4,112,384]{2,1,0:T(8,128)(2,1)S(1)} %get-tuple-element.111), channel_id=1, source_target_pairs={{0,16},{1,17},{2,18},{3,19},{4,20},{5,21},{6,22},{7,23},{8,24},{9,... | collective-permute-start | bytes 1032200 | tf_op jit(solution)/shard_map/ppermute | solution.py:650
  49.0 11.9 %shard_map.340 = (bf16[256,384]{1,0:T(8,128)(2,1)S(1)}, bf16[256,384]{1,0:T(8,128)(2,1)S(1)}, f32[384,512]{1,0:T(8,128)S(1)}) custom-call(s32[1]{0:T(128)} %bitcast.refs_0_, s32[1]{0:T(128)S(6)} %copy.39.refs_1_, bf16[512,384]{1,0:T(8,128)(2,1)S(1)} %get-tuple-element.70.refs_2_, bf16[1024,384]{1,0:T(8,128)(2,1)S(1)} %get-tuple-element.71.refs_3_.refs_5_, ...), custom_call_target="tpu_custom_call" | custom-call | flops 12999999488 | bytes 13000000 | tf_op jit(solution)/shard_map/pallas_call | solution.py:615
  61.0 2.1 %collective-permute-done.5 = bf16[4,112,384]{2,1,0:T(8,128)(2,1)S(1)} collective-permute-done((bf16[4,112,384]{2,1,0:T(8,128)(2,1)S(1)}, bf16[4,112,384]{2,1,0:T(8,128)(2,1)S(1)}, u32[]{:S(2)}, u32[]{:S(2)}) %collective-permute-start.5) | collective-permute-done | bytes 344096 | tf_op jit(solution)/shard_map/ppermute | solution.py:650
  64.2 2.4 %collective-permute-start.9 = (bf16[1,112,384]{2,1,0:T(8,128)(2,1)S(1)}, bf16[1,112,384]{2,1,0:T(8,128)(2,1)S(1)}, u32[]{:S(2)}, u32[]{:S(2)}) collective-permute-start(bf16[1,112,384]{2,1,0:T(8,128)(2,1)S(1)} %add_convert_fusion.8), channel_id=1, source_target_pairs={{0,4},{1,5},{2,6},{3,7},{4,0},{5,1},{6,2},{7,3},{8,12},{9,13},{10,... | collective-permute-start | bytes 258056 | tf_op jit(solution)/shard_map/ppermute | solution.py:650
  67.1 6.3 %shard_map.341 = (bf16[256,384]{1,0:T(8,128)(2,1)S(1)}, bf16[256,384]{1,0:T(8,128)(2,1)S(1)}, f32[384,512]{1,0:T(8,128)S(1)}) custom-call(s32[1]{0:T(128)} %bitcast.refs_0_, s32[1]{0:T(128)S(6)} %copy.39.refs_1_, bf16[512,384]{1,0:T(8,128)(2,1)S(1)} %get-tuple-element.70.refs_2_, bf16[1024,384]{1,0:T(8,128)(2,1)S(1)} %get-tuple-element.71.refs_3_.refs_5_, ...), custom_call_target="tpu_custom_call" | custom-call | flops 8000000000 | bytes 8000000 | tf_op jit(solution)/shard_map/pallas_call | solution.py:615
  73.6 4.7 %shard_map.343 = (f32[256,384]{1,0:T(8,128)}, bf16[512,384]{1,0:T(8,128)(2,1)}, bf16[512,384]{1,0:T(8,128)(2,1)}, bf16[1024,384]{1,0:T(8,128)(2,1)}) custom-call(s32[1]{0:T(128)} %bitcast.refs_0_, bf16[256,384]{1,0:T(8,128)(2,1)} %bitcast.35, bf16[512,384]{1,0:T(8,128)(2,1)} %refs_2_.3, bf16[256,384]{1,0:T(8,128)(2,1)S(1)} %get-tuple-element.80.refs_3_, ...), custom_call_target="tpu_custom_call" | custom-call | flops 4000000000 | bytes 4000000 | tf_op jit(solution)/shard_map/pallas_call | solution.py:615
  78.3 2.7 %collective-permute-start.14 = (bf16[8,64,384]{2,1,0:T(8,128)(2,1)}, bf16[8,64,384]{2,1,0:T(8,128)(2,1)S(1)}, u32[]{:S(2)}, u32[]{:S(2)}) collective-permute-start(bf16[8,64,384]{2,1,0:T(8,128)(2,1)} %bitcast.30), channel_id=1, source_target_pairs={{0,8},{1,9},{2,10},{3,11},{4,12},{5,13},{6,14},{7,15},{8,0},{9,1},... | collective-permute-start | bytes 1179656 | tf_op jit(solution)/shard_map/ppermute | solution.py:650
  88.5 1.9 %collective-permute-start.30 = (bf16[1,112,384]{2,1,0:T(8,128)(2,1)S(1)}, bf16[1,112,384]{2,1,0:T(8,128)(2,1)S(1)}, u32[]{:S(2)}, u32[]{:S(2)}) collective-permute-start(bf16[1,112,384]{2,1,0:T(8,128)(2,1)S(1)} %add_convert_fusion.6), channel_id=1, source_target_pairs={{0,4},{1,5},{2,6},{3,7},{4,0},{5,1},{6,2},{7,3},{8,12},{9,13},{10,... | collective-permute-start | bytes 258056 | tf_op jit(solution)/shard_map/ppermute | solution.py:650
  90.4 4.5 %collective-permute-done.16 = bf16[4,64,384]{2,1,0:T(8,128)(2,1)S(1)} collective-permute-done((bf16[4,64,384]{2,1,0:T(8,128)(2,1)S(1)}, bf16[4,64,384]{2,1,0:T(8,128)(2,1)S(1)}, u32[]{:S(2)}, u32[]{:S(2)}) %collective-permute-start.16) | collective-permute-done | bytes 196640 | tf_op jit(solution)/shard_map/ppermute | solution.py:650
  96.8 3.1 %collective-permute-start.20 = (bf16[1,64,384]{2,1,0:T(8,128)(2,1)S(1)}, bf16[1,64,384]{2,1,0:T(8,128)(2,1)S(1)}, u32[]{:S(2)}, u32[]{:S(2)}) collective-permute-start(bf16[1,64,384]{2,1,0:T(8,128)(2,1)S(1)} %add_convert_fusion.12), channel_id=1, source_target_pairs={{0,4},{1,5},{2,6},{3,7},{4,0},{5,1},{6,2},{7,3},{8,12},{9,13},{10,... | collective-permute-start | bytes 147464 | tf_op jit(solution)/shard_map/ppermute | solution.py:650
  101.9 2.5 %collective-permute-done.19 = bf16[1,64,384]{2,1,0:T(8,128)(2,1)S(1)} collective-permute-done((bf16[1,64,384]{2,1,0:T(8,128)(2,1)S(1)}, bf16[1,64,384]{2,1,0:T(8,128)(2,1)S(1)}, u32[]{:S(2)}, u32[]{:S(2)}) %collective-permute-start.19) | collective-permute-done | bytes 49184 | tf_op jit(solution)/shard_map/ppermute | solution.py:650
  105.8 4.3 %collective-permute-start.23 = (bf16[1,64,384]{2,1,0:T(8,128)(2,1)S(1)}, bf16[1,64,384]{2,1,0:T(8,128)(2,1)S(1)}, u32[]{:S(2)}, u32[]{:S(2)}) collective-permute-start(bf16[1,64,384]{2,1,0:T(8,128)(2,1)S(1)} %add_convert_fusion.10), channel_id=1, source_target_pairs={{0,4},{1,5},{2,6},{3,7},{4,0},{5,1},{6,2},{7,3},{8,12},{9,13},{10,... | collective-permute-start | bytes 147464 | tf_op jit(solution)/shard_map/ppermute | solution.py:650
  110.2 2.0 %collective-permute-start.34 = (bf16[4,112,384]{2,1,0:T(8,128)(2,1)S(1)}, bf16[4,112,384]{2,1,0:T(8,128)(2,1)S(1)}, u32[]{:S(2)}, u32[]{:S(2)}) collective-permute-start(bf16[4,112,384]{2,1,0:T(8,128)(2,1)S(1)} %pad_maximum_fusion.2), channel_id=1, source_target_pairs={{0,17},{1,16},{2,19},{3,18},{4,21},{5,20},{6,23},{7,22},{8,25},{9,... | collective-permute-start | bytes 1032200 | tf_op jit(solution)/shard_map/ppermute | solution.py:650
  115.8 1.6 %collective-permute-done.34 = bf16[4,112,384]{2,1,0:T(8,128)(2,1)S(1)} collective-permute-done((bf16[4,112,384]{2,1,0:T(8,128)(2,1)S(1)}, bf16[4,112,384]{2,1,0:T(8,128)(2,1)S(1)}, u32[]{:S(2)}, u32[]{:S(2)}) %collective-permute-start.34) | collective-permute-done | bytes 344096 | tf_op jit(solution)/shard_map/ppermute | solution.py:650
  118.4 5.8 %collective-permute-done.33 = bf16[4,112,384]{2,1,0:T(8,128)(2,1)S(1)} collective-permute-done((bf16[4,112,384]{2,1,0:T(8,128)(2,1)S(1)}, bf16[4,112,384]{2,1,0:T(8,128)(2,1)S(1)}, u32[]{:S(2)}, u32[]{:S(2)}) %collective-permute-start.33) | collective-permute-done | bytes 344096 | tf_op jit(solution)/shard_map/ppermute | solution.py:650
  124.1 2.8 %collective-permute-done.32 = bf16[4,112,384]{2,1,0:T(8,128)(2,1)S(1)} collective-permute-done((bf16[4,112,384]{2,1,0:T(8,128)(2,1)S(1)}, bf16[4,112,384]{2,1,0:T(8,128)(2,1)S(1)}, u32[]{:S(2)}, u32[]{:S(2)}) %collective-permute-start.32) | collective-permute-done | bytes 344096 | tf_op jit(solution)/shard_map/ppermute | solution.py:650
  127.4 6.2 %collective-permute-start.35 = (bf16[16,112,384]{2,1,0:T(8,128)(2,1)S(1)}, bf16[16,112,384]{2,1,0:T(8,128)(2,1)S(1)}, u32[]{:S(2)}, u32[]{:S(2)}) collective-permute-start(bf16[16,112,384]{2,1,0:T(8,128)(2,1)S(1)} %pad_maximum_fusion), channel_id=1, source_target_pairs={{0,8},{1,9},{2,10},{3,11},{4,12},{5,13},{6,14},{7,15},{8,0},{9,1},... | collective-permute-start | bytes 4128776 | tf_op jit(solution)/shard_map/ppermute | solution.py:650
  133.9 4.0 %collective-permute-start.28 = (bf16[16,64,384]{2,1,0:T(8,128)(2,1)S(1)}, bf16[16,64,384]{2,1,0:T(8,128)(2,1)}, u32[]{:S(2)}, u32[]{:S(2)}) collective-permute-start(bf16[16,64,384]{2,1,0:T(8,128)(2,1)S(1)} %pad_maximum_fusion.1), channel_id=1, source_target_pairs={{0,8},{1,9},{2,10},{3,11},{4,12},{5,13},{6,14},{7,15},{8,0},{9,1},... | collective-permute-start | bytes 2359304 | tf_op jit(solution)/shard_map/ppermute | solution.py:650
  137.9 2.0 %collective-permute-done.28 = bf16[16,64,384]{2,1,0:T(8,128)(2,1)} collective-permute-done((bf16[16,64,384]{2,1,0:T(8,128)(2,1)S(1)}, bf16[16,64,384]{2,1,0:T(8,128)(2,1)}, u32[]{:S(2)}, u32[]{:S(2)}) %collective-permute-start.28) | collective-permute-done | bytes 786464 | tf_op jit(solution)/shard_map/ppermute | solution.py:650
  139.9 4.8 %shard_map.344 = (f32[384,384]{1,0:T(8,128)}, f32[384]{0:T(512)}, f32[384,384]{1,0:T(8,128)}, f32[384]{0:T(512)}, f32[384,384]{1,0:T(8,128)}, /*index=5*/f32[384]{0:T(512)}, f32[512,384]{1,0:T(8,128)}) custom-call(s32[1]{0:T(128)} %bitcast.8.refs_0_, bf16[1024,384]{1,0:T(8,128)(2,1)S(1)} %bitcast.17, bf16[1024,384]{1,0:T(8,128)(2,1)} %bitcast.13.refs_2_), custom_call_target="tpu_custom_call" | custom-call | flops 2000000000 | bytes 2000000 | tf_op jit(solution)/shard_map/pallas_call | solution.py:615
  144.7 3.3 %shard_map.345 = (f32[1536,384]{1,0:T(8,128)}, f32[384,1536]{1,0:T(8,128)}, f32[384,384]{1,0:T(8,128)}, f32[384]{0:T(512)}, f32[384]{0:T(512)}, /*index=5*/f32[3...) custom-call(s32[1]{0:T(128)} %bitcast.8.refs_0_, bf16[1792,384]{1,0:T(8,128)(2,1)S(1)} %bitcast.16, ...), custom_call_target="tpu_custom_call" | custom-call | flops 4000000000 | bytes 4000000 | tf_op jit(solution)/shard_map/pallas_call | solution.py:615
  (74 shorter events, 29.2 us)
Async XLA Ops:
  2.0 7.0 %collective-permute-start = (bf16[256,384]{1,0:T(8,128)(2,1)}, bf16[256,384]{1,0:T(8,128)(2,1)S(1)}, u32[]{:S(2)}, u32[]{:S(2)}) collective-permute-start(bf16[256,384]{1,0:T(8,128)(2,1)} %bitcast.33), channel_id=1, source_target_pairs={{0,8},{8,0},{16,24},{24,16},{1,9},{9,1},{17,25},{25,17},{2,10},{10... | collective-permute-start | bytes 589832 | tf_op jit(solution)/shard_map/ppermute | solution.py:783
  34.3 14.5 %collective-permute-start.13 = (bf16[256,512]{1,0:T(8,128)(2,1)S(1)}, bf16[256,512]{1,0:T(8,128)(2,1)S(1)}, u32[]{:S(2)}, u32[]{:S(2)}) collective-permute-start(bf16[256,512]{1,0:T(8,128)(2,1)S(1)} %get-tuple-element.75.refs_7_.refs_3_), channel_id=1, source_target_pairs={{0,24},{8,16},{16,8},{24,0},{1,25},{9,17},{17,9},{25,1},{2,26},{10... | collective-permute-start | bytes 786440 | tf_op jit(solution)/shard_map/ppermute | solution.py:783
  35.8 13.2 %collective-permute-start.12 = (bf16[256,512]{1,0:T(8,128)(2,1)S(1)}, bf16[256,512]{1,0:T(8,128)(2,1)S(1)}, u32[]{:S(2)}, u32[]{:S(2)}) collective-permute-start(bf16[256,512]{1,0:T(8,128)(2,1)S(1)} %get-tuple-element.75.refs_7_.refs_3_), channel_id=1, source_target_pairs={{0,16},{8,24},{16,0},{24,8},{1,17},{9,25},{17,1},{25,9},{2,18},{10... | collective-permute-start | bytes 786440 | tf_op jit(solution)/shard_map/ppermute | solution.py:783
  37.1 11.9 %collective-permute-start.11 = (bf16[256,512]{1,0:T(8,128)(2,1)S(1)}, bf16[256,512]{1,0:T(8,128)(2,1)S(1)}, u32[]{:S(2)}, u32[]{:S(2)}) collective-permute-start(bf16[256,512]{1,0:T(8,128)(2,1)S(1)} %get-tuple-element.75.refs_7_.refs_3_), channel_id=1, source_target_pairs={{0,8},{8,0},{16,24},{24,16},{1,9},{9,1},{17,25},{25,17},{2,10},{10... | collective-permute-start | bytes 786440 | tf_op jit(solution)/shard_map/ppermute | solution.py:783
  37.1 8.3 %collective-permute-start.3 = (bf16[8,112,384]{2,1,0:T(8,128)(2,1)}, bf16[8,112,384]{2,1,0:T(8,128)(2,1)S(1)}, u32[]{:S(2)}, u32[]{:S(2)}) collective-permute-start(bf16[8,112,384]{2,1,0:T(8,128)(2,1)} %bitcast.28), channel_id=1, source_target_pairs={{0,8},{1,9},{2,10},{3,11},{4,12},{5,13},{6,14},{7,15},{8,0},{9,1},... | collective-permute-start | bytes 2064392 | tf_op jit(solution)/shard_map/ppermute | solution.py:650
  37.7 7.8 %collective-permute-start.4 = (bf16[8,112,384]{2,1,0:T(8,128)(2,1)}, bf16[8,112,384]{2,1,0:T(8,128)(2,1)S(1)}, u32[]{:S(2)}, u32[]{:S(2)}) collective-permute-start(bf16[8,112,384]{2,1,0:T(8,128)(2,1)} %bitcast.27), channel_id=1, source_target_pairs={{0,8},{1,9},{2,10},{3,11},{4,12},{5,13},{6,14},{7,15},{8,0},{9,1},... | collective-permute-start | bytes 2064392 | tf_op jit(solution)/shard_map/ppermute | solution.py:650
  45.9 17.1 %collective-permute-start.5 = (bf16[4,112,384]{2,1,0:T(8,128)(2,1)S(1)}, bf16[4,112,384]{2,1,0:T(8,128)(2,1)S(1)}, u32[]{:S(2)}, u32[]{:S(2)}) collective-permute-start(bf16[4,112,384]{2,1,0:T(8,128)(2,1)S(1)} %get-tuple-element.111), channel_id=1, source_target_pairs={{0,16},{1,17},{2,18},{3,19},{4,20},{5,21},{6,22},{7,23},{8,24},{9,... | collective-permute-start | bytes 1032200 | tf_op jit(solution)/shard_map/ppermute | solution.py:650
  47.8 15.3 %collective-permute-start.7 = (bf16[4,112,384]{2,1,0:T(8,128)(2,1)S(1)}, bf16[4,112,384]{2,1,0:T(8,128)(2,1)S(1)}, u32[]{:S(2)}, u32[]{:S(2)}) collective-permute-start(bf16[4,112,384]{2,1,0:T(8,128)(2,1)S(1)} %get-tuple-element.112), channel_id=1, source_target_pairs={{0,17},{1,16},{2,19},{3,18},{4,21},{5,20},{6,23},{7,22},{8,25},{9,... | collective-permute-start | bytes 1032200 | tf_op jit(solution)/shard_map/ppermute | solution.py:650
  48.8 15.3 %collective-permute-start.6 = (bf16[4,112,384]{2,1,0:T(8,128)(2,1)S(1)}, bf16[4,112,384]{2,1,0:T(8,128)(2,1)S(1)}, u32[]{:S(2)}, u32[]{:S(2)}) collective-permute-start(bf16[4,112,384]{2,1,0:T(8,128)(2,1)S(1)} %get-tuple-element.113), channel_id=1, source_target_pairs={{0,1},{1,0},{2,3},{3,2},{4,5},{5,4},{6,7},{7,6},{8,9},{9,8},{10,11... | collective-permute-start | bytes 1032200 | tf_op jit(solution)/shard_map/ppermute | solution.py:650
  64.2 9.2 %collective-permute-start.9 = (bf16[1,112,384]{2,1,0:T(8,128)(2,1)S(1)}, bf16[1,112,384]{2,1,0:T(8,128)(2,1)S(1)}, u32[]{:S(2)}, u32[]{:S(2)}) collective-permute-start(bf16[1,112,384]{2,1,0:T(8,128)(2,1)S(1)} %add_convert_fusion.8), channel_id=1, source_target_pairs={{0,4},{1,5},{2,6},{3,7},{4,0},{5,1},{6,2},{7,3},{8,12},{9,13},{10,... | collective-permute-start | bytes 258056 | tf_op jit(solution)/shard_map/ppermute | solution.py:650
  84.5 10.4 %collective-permute-start.16 = (bf16[4,64,384]{2,1,0:T(8,128)(2,1)S(1)}, bf16[4,64,384]{2,1,0:T(8,128)(2,1)S(1)}, u32[]{:S(2)}, u32[]{:S(2)}) collective-permute-start(bf16[4,64,384]{2,1,0:T(8,128)(2,1)S(1)} %get-tuple-element.116), channel_id=1, source_target_pairs={{0,16},{1,17},{2,18},{3,19},{4,20},{5,21},{6,22},{7,23},{8,24},{9,... | collective-permute-start | bytes 589832 | tf_op jit(solution)/shard_map/ppermute | solution.py:650
  85.5 10.4 %collective-permute-start.18 = (bf16[4,64,384]{2,1,0:T(8,128)(2,1)S(1)}, bf16[4,64,384]{2,1,0:T(8,128)(2,1)S(1)}, u32[]{:S(2)}, u32[]{:S(2)}) collective-permute-start(bf16[4,64,384]{2,1,0:T(8,128)(2,1)S(1)} %get-tuple-element.117), channel_id=1, source_target_pairs={{0,17},{1,16},{2,19},{3,18},{4,21},{5,20},{6,23},{7,22},{8,25},{9,... | collective-permute-start | bytes 589832 | tf_op jit(solution)/shard_map/ppermute | solution.py:650
  86.9 9.0 %collective-permute-start.17 = (bf16[4,64,384]{2,1,0:T(8,128)(2,1)S(1)}, bf16[4,64,384]{2,1,0:T(8,128)(2,1)S(1)}, u32[]{:S(2)}, u32[]{:S(2)}) collective-permute-start(bf16[4,64,384]{2,1,0:T(8,128)(2,1)S(1)} %get-tuple-element.118), channel_id=1, source_target_pairs={{0,1},{1,0},{2,3},{3,2},{4,5},{5,4},{6,7},{7,6},{8,9},{9,8},{10,11... | collective-permute-start | bytes 589832 | tf_op jit(solution)/shard_map/ppermute | solution.py:650
  87.2 14.2 %collective-permute-start.31 = (bf16[1,112,384]{2,1,0:T(8,128)(2,1)S(1)}, bf16[1,112,384]{2,1,0:T(8,128)(2,1)S(1)}, u32[]{:S(2)}, u32[]{:S(2)}) collective-permute-start(bf16[1,112,384]{2,1,0:T(8,128)(2,1)S(1)} %add_convert_fusion.6), channel_id=1, source_target_pairs={{0,6},{1,7},{2,4},{3,5},{4,2},{5,3},{6,0},{7,1},{8,14},{9,15},{10,... | collective-permute-start | bytes 258056 | tf_op jit(solution)/shard_map/ppermute | solution.py:650
  88.5 13.0 %collective-permute-start.30 = (bf16[1,112,384]{2,1,0:T(8,128)(2,1)S(1)}, bf16[1,112,384]{2,1,0:T(8,128)(2,1)S(1)}, u32[]{:S(2)}, u32[]{:S(2)}) collective-permute-start(bf16[1,112,384]{2,1,0:T(8,128)(2,1)S(1)} %add_convert_fusion.6), channel_id=1, source_target_pairs={{0,4},{1,5},{2,6},{3,7},{4,0},{5,1},{6,2},{7,3},{8,12},{9,13},{10,... | collective-permute-start | bytes 258056 | tf_op jit(solution)/shard_map/ppermute | solution.py:650
  105.3 7.2 %collective-permute-start.24 = (bf16[1,64,384]{2,1,0:T(8,128)(2,1)S(1)}, bf16[1,64,384]{2,1,0:T(8,128)(2,1)S(1)}, u32[]{:S(2)}, u32[]{:S(2)}) collective-permute-start(bf16[1,64,384]{2,1,0:T(8,128)(2,1)S(1)} %add_convert_fusion.10), channel_id=1, source_target_pairs={{0,6},{1,7},{2,4},{3,5},{4,2},{5,3},{6,0},{7,1},{8,14},{9,15},{10,... | collective-permute-start | bytes 147464 | tf_op jit(solution)/shard_map/ppermute | solution.py:650
  105.8 7.1 %collective-permute-start.23 = (bf16[1,64,384]{2,1,0:T(8,128)(2,1)S(1)}, bf16[1,64,384]{2,1,0:T(8,128)(2,1)S(1)}, u32[]{:S(2)}, u32[]{:S(2)}) collective-permute-start(bf16[1,64,384]{2,1,0:T(8,128)(2,1)S(1)} %add_convert_fusion.10), channel_id=1, source_target_pairs={{0,4},{1,5},{2,6},{3,7},{4,0},{5,1},{6,2},{7,3},{8,12},{9,13},{10,... | collective-permute-start | bytes 147464 | tf_op jit(solution)/shard_map/ppermute | solution.py:650
  110.2 7.2 %collective-permute-start.34 = (bf16[4,112,384]{2,1,0:T(8,128)(2,1)S(1)}, bf16[4,112,384]{2,1,0:T(8,128)(2,1)S(1)}, u32[]{:S(2)}, u32[]{:S(2)}) collective-permute-start(bf16[4,112,384]{2,1,0:T(8,128)(2,1)S(1)} %pad_maximum_fusion.2), channel_id=1, source_target_pairs={{0,17},{1,16},{2,19},{3,18},{4,21},{5,20},{6,23},{7,22},{8,25},{9,... | collective-permute-start | bytes 1032200 | tf_op jit(solution)/shard_map/ppermute | solution.py:650
  112.2 11.9 %collective-permute-start.33 = (bf16[4,112,384]{2,1,0:T(8,128)(2,1)S(1)}, bf16[4,112,384]{2,1,0:T(8,128)(2,1)S(1)}, u32[]{:S(2)}, u32[]{:S(2)}) collective-permute-start(bf16[4,112,384]{2,1,0:T(8,128)(2,1)S(1)} %pad_maximum_fusion.2), channel_id=1, source_target_pairs={{0,1},{1,0},{2,3},{3,2},{4,5},{5,4},{6,7},{7,6},{8,9},{9,8},{10,11... | collective-permute-start | bytes 1032200 | tf_op jit(solution)/shard_map/ppermute | solution.py:650
  112.4 14.5 %collective-permute-start.32 = (bf16[4,112,384]{2,1,0:T(8,128)(2,1)S(1)}, bf16[4,112,384]{2,1,0:T(8,128)(2,1)S(1)}, u32[]{:S(2)}, u32[]{:S(2)}) collective-permute-start(bf16[4,112,384]{2,1,0:T(8,128)(2,1)S(1)} %pad_maximum_fusion.2), channel_id=1, source_target_pairs={{0,16},{1,17},{2,18},{3,19},{4,20},{5,21},{6,22},{7,23},{8,24},{9,... | collective-permute-start | bytes 1032200 | tf_op jit(solution)/shard_map/ppermute | solution.py:650
  113.6 20.0 %collective-permute-start.26 = (bf16[4,64,384]{2,1,0:T(8,128)(2,1)S(1)}, bf16[4,64,384]{2,1,0:T(8,128)(2,1)S(1)}, u32[]{:S(2)}, u32[]{:S(2)}) collective-permute-start(bf16[4,64,384]{2,1,0:T(8,128)(2,1)S(1)} %pad_maximum_fusion.3), channel_id=1, source_target_pairs={{0,1},{1,0},{2,3},{3,2},{4,5},{5,4},{6,7},{7,6},{8,9},{9,8},{10,11... | collective-permute-start | bytes 589832 | tf_op jit(solution)/shard_map/ppermute | solution.py:650
  114.9 18.7 %collective-permute-start.27 = (bf16[4,64,384]{2,1,0:T(8,128)(2,1)S(1)}, bf16[4,64,384]{2,1,0:T(8,128)(2,1)S(1)}, u32[]{:S(2)}, u32[]{:S(2)}) collective-permute-start(bf16[4,64,384]{2,1,0:T(8,128)(2,1)S(1)} %pad_maximum_fusion.3), channel_id=1, source_target_pairs={{0,17},{1,16},{2,19},{3,18},{4,21},{5,20},{6,23},{7,22},{8,25},{9,... | collective-permute-start | bytes 589832 | tf_op jit(solution)/shard_map/ppermute | solution.py:650
  117.4 16.2 %collective-permute-start.25 = (bf16[4,64,384]{2,1,0:T(8,128)(2,1)S(1)}, bf16[4,64,384]{2,1,0:T(8,128)(2,1)S(1)}, u32[]{:S(2)}, u32[]{:S(2)}) collective-permute-start(bf16[4,64,384]{2,1,0:T(8,128)(2,1)S(1)} %pad_maximum_fusion.3), channel_id=1, source_target_pairs={{0,16},{1,17},{2,18},{3,19},{4,20},{5,21},{6,22},{7,23},{8,24},{9,... | collective-permute-start | bytes 589832 | tf_op jit(solution)/shard_map/ppermute | solution.py:650
  127.4 17.3 %collective-permute-start.35 = (bf16[16,112,384]{2,1,0:T(8,128)(2,1)S(1)}, bf16[16,112,384]{2,1,0:T(8,128)(2,1)S(1)}, u32[]{:S(2)}, u32[]{:S(2)}) collective-permute-start(bf16[16,112,384]{2,1,0:T(8,128)(2,1)S(1)} %pad_maximum_fusion), channel_id=1, source_target_pairs={{0,8},{1,9},{2,10},{3,11},{4,12},{5,13},{6,14},{7,15},{8,0},{9,1},... | collective-permute-start | bytes 4128776 | tf_op jit(solution)/shard_map/ppermute | solution.py:650
  (13 other events, 63.5 us)
